TPU v7x, 32 devices: a whole 2x2x4 slice. The times are simulated.
32 devices in a mesh: shot: 8 (over z, y), dom: 4 (over x, core).
Axes of the slice: x: 2, y: 2, z: 4, core: 2. Of those that a mesh axis runs over, the one named last changes fastest.
Arguments:
- coefficient: float32 [128, 16, 384], P('dom'), may hold values from 0.02 to 0.18
- fwd_older: float32 [8, 128, 16, 384], P('shot', 'dom'), may hold values from -6 to 6
- fwd_recent: float32 [8, 128, 16, 384], P('shot', 'dom'), may hold values from -6 to 6
- adj_later: float32 [8, 128, 16, 384], P('shot', 'dom'), may hold values from -6 to 6
- adj_recent: float32 [8, 128, 16, 384], P('shot', 'dom'), may hold values from -6 to 6
- source_xcell: int32 [8], P('shot'), may hold values from 0 to 127
- source_ycell: int32 [8], P('shot'), may hold values from 0 to 15
- source_zcell: int32 [8], P('shot'), may hold values from 0 to 383
- amplitude: float32 [8, 2], P('shot'), may hold values from 1773.62 to 3547.24
- receiver_xcell: int32 [8, 1024], P('shot'), may hold values from 0 to 127
- receiver_ycell: int32 [8, 1024], P('shot'), may hold values from 0 to 15
- receiver_zcell: int32 [8, 1024], P('shot'), may hold values from 0 to 383
- observed: float32 [8, 2, 1024], P('shot'), may hold values from -6 to 6
Outputs:
- fwd_latest: float32 [8, 128, 16, 384], P('shot', 'dom')
- adj_latest: float32 [8, 128, 16, 384], P('shot', 'dom')
- model_gradient: float32 [128, 16, 384], P('dom')
All inputs are finite; a program needn't handle non-finite values.
Results may differ from a plain program's by a relative error of at most 0.0003.
Values sent between devices are 32-bit elements; how exact they have to be, the bound alone decides.
A program may use at most 64 MiB of HBM per device.

v0:
```python
import jax
import jax.numpy as jnp
from jax import lax
from jax.sharding import PartitionSpec as P

R = 4


stencil_weights = (-205.0 / 72.0, 8.0 / 5.0, -1.0 / 5.0, 8.0 / 315.0, -1.0 / 560.0)


def with_halo(block, sides, width):
    for axis, dim in sides:
        count = lax.axis_size(axis)
        forward = [(i, i + 1) for i in range(count - 1)]
        backward = [(target, source) for source, target in forward]
        low = lax.ppermute(
            lax.slice_in_dim(block, block.shape[dim] - width, None, axis=dim), axis, forward
        )
        high = lax.ppermute(lax.slice_in_dim(block, 0, width, axis=dim), axis, backward)
        block = jnp.concatenate([low, block, high], axis=dim)
    return block


def laplace_core(extended):
    count = extended.shape[0] - 2 * R
    center = extended[R : R + count]
    width_y = center.shape[1]
    width_z = center.shape[2]
    total = 3.0 * stencil_weights[0] * center
    padded = jnp.pad(center, ((0, 0), (R, R), (R, R)))
    for offset in range(1, R + 1):
        weight = stencil_weights[offset]
        total = total + weight * (
            extended[R + offset : R + offset + count] + extended[R - offset : R - offset + count]
        )
        total = total + weight * (
            padded[:, R + offset : R + offset + width_y, R : R + width_z]
            + padded[:, R - offset : R - offset + width_y, R : R + width_z]
        )
        total = total + weight * (
            padded[:, R : R + width_y, R + offset : R + offset + width_z]
            + padded[:, R : R + width_y, R - offset : R - offset + width_z]
        )
    return total


def point_grid(shape, xcells, ycells, zcells, values, start):
    count = shape[0]
    inside = (xcells >= start) & (xcells < start + count)
    local = jnp.clip(xcells - start, 0, count - 1)
    kept = jnp.where(inside, values, jnp.zeros_like(values))
    return jnp.zeros(shape, values.dtype).at[local, ycells, zcells].add(kept)


def sample(field, xcells, ycells, zcells, start):
    count = field.shape[0]
    inside = (xcells >= start) & (xcells < start + count)
    local = jnp.clip(xcells - start, 0, count - 1)
    picked = field[local, ycells, zcells]
    return jnp.where(inside, picked, jnp.zeros_like(picked))


def shards(
    coefficient,
    fwd_older,
    fwd_recent,
    adj_later,
    adj_recent,
    source_xcell,
    source_ycell,
    source_zcell,
    amplitude,
    receiver_xcell,
    receiver_ycell,
    receiver_zcell,
    observed,
):
    count = coefficient.shape[0]
    shape = coefficient.shape
    base = lax.axis_index("dom") * count
    older = fwd_older[0]
    recent = fwd_recent[0]
    later = adj_later[0]
    adj_now = adj_recent[0]
    rxc = receiver_xcell[0]
    ryc = receiver_ycell[0]
    rzc = receiver_zcell[0]

    def advance(current, before, sources):
        extended = with_halo(current, (("dom", 0),), R)
        return 2.0 * current - before + coefficient * (laplace_core(extended) + sources)

    fwd_two = advance(
        recent,
        older,
        point_grid(shape, source_xcell, source_ycell, source_zcell, amplitude[0, 0:1], base),
    )
    fwd_three = advance(
        fwd_two,
        recent,
        point_grid(shape, source_xcell, source_ycell, source_zcell, amplitude[0, 1:2], base),
    )
    samples = jnp.stack(
        [sample(fwd_two, rxc, ryc, rzc, base), sample(fwd_three, rxc, ryc, rzc, base)]
    )
    traces = lax.psum(samples, "dom")
    resid_two = traces[0] - observed[0, 0]
    resid_three = traces[1] - observed[0, 1]
    adj_two = advance(adj_now, later, point_grid(shape, rxc, ryc, rzc, resid_three, base))
    late_term = adj_two * (fwd_three - 2.0 * fwd_two + recent)
    adj_one = advance(adj_two, adj_now, point_grid(shape, rxc, ryc, rzc, resid_two, base))
    early_term = adj_one * (fwd_two - 2.0 * recent + older)
    gradient = lax.psum(early_term + late_term, "shot")
    return (fwd_three[None], adj_one[None], gradient)


def solution(mesh):
    return jax.shard_map(
        shards,
        mesh=mesh,
        in_specs=(
            P("dom", None, None),
            P("shot", "dom", None, None),
            P("shot", "dom", None, None),
            P("shot", "dom", None, None),
            P("shot", "dom", None, None),
            P("shot"),
            P("shot"),
            P("shot"),
            P("shot", None),
            P("shot", None),
            P("shot", None),
            P("shot", None),
            P("shot", None, None),
        ),
        out_specs=(
            P("shot", "dom", None, None),
            P("shot", "dom", None, None),
            P("dom", None, None),
        ),
        check_vma=False,
    )
```

profile of v0, /device:TPU:0, one launch (start us, length us, event | category | flops | bytes accessed | tf_op | source)
XLA Modules:
  0.0 198.1 jit_solution(6927947139560722236)
XLA Ops:
  7.2 0.0 copy-start.14
  7.2 0.0 copy-start.12
  7.2 0.0 copy-start.13
  7.2 0.0 copy-start.1
  7.3 0.0 all-reduce.6.cloned.1.call-start
  7.3 1.7 slice_bitcast_fusion.1
  9.0 1.3 collective-permute-start.4
  10.3 3.0 %collective-permute-start.5 = (f32[4,16,384]{2,1,0:T(8,128)}, f32[4,16,384]{2,1,0:T(8,128)S(1)}, u32[]{:S(2)}, u32[]{:S(2)}) collective-permute-start(f32[4,16,384]{2,1,0:T(8,128)} %get-tuple-element.34), channel_id=1, source_target_pairs={{0,1},{1,2},{2,3},{4,5},{5,6},{6,7},{8,9},{9,10},{10,11},{12,13},{... | collective-permute-start | bytes 294920 | tf_op jit(solution)/shard_map/ppermute | solution.py:17
  13.3 1.0 slice_bitcast_fusion.3
  14.3 1.3 collective-permute-start
  15.6 5.1 %collective-permute-start.1 = (f32[4,16,384]{2,1,0:T(8,128)S(1)}, f32[4,16,384]{2,1,0:T(8,128)S(1)}, u32[]{:S(2)}, u32[]{:S(2)}) collective-permute-start(f32[4,16,384]{2,1,0:T(8,128)S(1)} %get-tuple-element.38), channel_id=1, source_target_pairs={{0,1},{1,2},{2,3},{4,5},{5,6},{6,7},{8,9},{9,10},{10,11},{12,13},{... | collective-permute-start | bytes 294920 | tf_op jit(solution)/shard_map/ppermute | solution.py:17
  22.6 0.6 fusion.178
  24.6 0.7 and_reduce_fusion.1
  26.6 0.0 copy-done.7
  26.6 0.6 fusion.176
  27.2 0.0 copy-done.5
  27.2 0.0 copy-done.8
  27.2 0.1 and_reduce_fusion
  27.3 0.1 multiply_reduce_fusion
  27.4 0.6 fusion.172
  28.1 0.0 collective-permute-done
  28.1 0.0 collective-permute-done.1
  28.1 0.0 copy-start.2
  28.1 2.7 %fusion.80 = f32[32,16,384]{2,1,0:T(8,128)S(1)} fusion(f32[32,16,384]{2,1,0:T(8,128)S(1)} %bitcast.66, f32[4,16,384]{2,1,0:T(8,128)S(1)} %collective-permute-done.1, f32[4,16,384]{2,1,0:T(8,128)S(1)} %collective-permute-done), kind=kLoop, calls=%fused_computation.196 | loop fusion | flops 8847360 | bytes 1769472 | tf_op jit(solution)/shard_map/add | solution.py:41
  30.8 0.6 add.438
  32.1 0.1 add.441
  32.2 0.0 copy-start.3
  32.2 1.4 fusion.169
  33.6 0.7 fusion.175
  34.3 1.3 collective-permute-start.2
  35.6 4.3 %collective-permute-start.3 = (f32[4,16,384]{2,1,0:T(8,128)}, f32[4,16,384]{2,1,0:T(8,128)S(1)}, u32[]{:S(2)}, u32[]{:S(2)}) collective-permute-start(f32[4,16,384]{2,1,0:T(8,128)} %get-tuple-element.36), channel_id=1, source_target_pairs={{0,1},{1,2},{2,3},{4,5},{5,6},{6,7},{8,9},{9,10},{10,11},{12,13},{... | collective-permute-start | bytes 294920 | tf_op jit(solution)/shard_map/ppermute | solution.py:17
  39.9 0.0 collective-permute-done.4
  39.9 0.0 collective-permute-done.5
  39.9 2.7 %fusion.32 = f32[32,16,384]{2,1,0:T(8,128)S(1)} fusion(f32[32,16,384]{2,1,0:T(8,128)S(1)} %bitcast.67, f32[4,16,384]{2,1,0:T(8,128)S(1)} %collective-permute-done.5, f32[4,16,384]{2,1,0:T(8,128)S(1)} %collective-permute-done.4), kind=kLoop, calls=%fused_computation.148 | loop fusion | flops 8847360 | bytes 1769472 | tf_op jit(solution)/shard_map/add | solution.py:41
  42.7 10.6 %gather_fusion = f32[1024]{0:T(1024)S(1)} fusion(f32[32,16,384]{2,1,0:T(8,128)S(1)} %fusion.169, s32[1024]{0:T(1024)S(1)} %bitcast.63), kind=kCustom, calls=%fused_computation | custom fusion | bytes 20480 | tf_op jit(solution)/shard_map/gather | solution.py:60
  53.2 0.1 reshape.178
  53.3 0.0 collective-permute-done.2
  53.3 0.0 collective-permute-done.3
  53.3 3.5 %fusion.56 = f32[32,16,384]{2,1,0:T(8,128)} fusion(f32[32,16,384]{2,1,0:T(8,128)S(1)} %fusion.169, f32[4,16,384]{2,1,0:T(8,128)S(1)} %collective-permute-done.3, f32[4,16,384]{2,1,0:T(8,128)S(1)} %collective-permute-done.2), kind=kLoop, calls=%fused_computation.172 | loop fusion | flops 8847360 | bytes 1769472 | tf_op jit(solution)/shard_map/add | solution.py:41
  56.8 1.3 add.467
  58.7 1.4 add.469
  60.1 1.6 multiply_add_fusion.1
  61.7 0.0 copy-start
  61.7 0.0 copy-start.6
  61.7 0.0 copy-start.10
  61.7 10.6 %gather_fusion.1 = f32[1024]{0:T(1024)S(1)} fusion(f32[32,16,384]{2,1,0:T(8,128)S(1)} %multiply_add_fusion.1, s32[1024]{0:T(1024)S(1)} %bitcast.64), kind=kCustom, calls=%fused_computation.1 | custom fusion | bytes 20480 | tf_op jit(solution)/shard_map/gather | solution.py:60
  72.3 7.5 %psum.14 = f32[2,1024]{1,0:T(2,128)S(1)} all-reduce(f32[2,1024]{1,0:T(2,128)S(1)} %pad_maximum_fusion.8), channel_id=1, replica_groups=mesh['shot'=8,'dom'=4] {'dom'}, use_global_device_ids=true, to_apply=%region_1.2 | all-reduce | flops 2048 | bytes 16384 | tf_op jit(solution)/shard_map/psum | solution.py:107
  79.9 6.4 %scatter_fusion = f32[196608]{0:T(1024)S(1)} fusion(f32[196608]{0:T(1024)S(1)} %reshape.178, s32[1024]{0:T(1024)S(1)} %broadcast_select_fusion, f32[1024]{0:T(1024)S(1)} %get-tuple-element.48), kind=kCustom, calls=%fused_computation.2 | custom fusion | flops 1024 | bytes 16384
  86.2 1.1 reshape.180
  87.3 2.0 %fusion.168 = f32[32,16,384]{2,1,0:T(8,128)S(1)} fusion(f32[1,32,16,384]{3,2,1,0:T(8,128)} %param.20, f32[32,16,384]{2,1,0:T(8,128)} %param.17, f32[32,16,384]{2,1,0:T(8,128)} %reshape.180, f32[1,32,16,384]{3,2,1,0:T(8,128)} %param.21), kind=kLoop, calls=%fused_computation.293 | loop fusion | flops 786432 | bytes 3932160 | tf_op jit(solution)/shard_map/add | solution.py:92
  89.3 0.0 copy-start.4
  89.4 1.3 collective-permute-start.6
  90.7 3.0 %collective-permute-start.7 = (f32[4,16,384]{2,1,0:T(8,128)S(1)}, f32[4,16,384]{2,1,0:T(8,128)S(1)}, u32[]{:S(2)}, u32[]{:S(2)}) collective-permute-start(f32[4,16,384]{2,1,0:T(8,128)S(1)} %get-tuple-element.32), channel_id=1, source_target_pairs={{0,1},{1,2},{2,3},{4,5},{5,6},{6,7},{8,9},{9,10},{10,11},{12,13},{... | collective-permute-start | bytes 294920 | tf_op jit(solution)/shard_map/ppermute | solution.py:17
  93.7 0.0 collective-permute-done.6
  93.7 0.9 collective-permute-done.7
  94.6 0.0 copy-done.4
  94.6 3.4 %fusion.8 = f32[32,16,384]{2,1,0:T(8,128)} fusion(f32[32,16,384]{2,1,0:T(8,128)S(1)} %fusion.168, f32[4,16,384]{2,1,0:T(8,128)S(1)} %collective-permute-done.7, f32[4,16,384]{2,1,0:T(8,128)S(1)} %collective-permute-done.6), kind=kLoop, calls=%fused_computation.124 | loop fusion | flops 8847360 | bytes 1769472 | tf_op jit(solution)/shard_map/add | solution.py:41
  98.1 1.2 reshape.182
  99.3 6.4 %scatter_fusion.1 = f32[196608]{0:T(1024)S(1)} fusion(f32[196608]{0:T(1024)S(1)} %reshape.182, s32[1024]{0:T(1024)S(1)} %broadcast_select_fusion, f32[1024]{0:T(1024)S(1)} %get-tuple-element.47), kind=kCustom, calls=%fused_computation.3 | custom fusion | flops 1024 | bytes 16384
  105.6 1.1 reshape.184
  106.7 3.6 %fusion.171 = (f32[32,16,384]{2,1,0:T(8,128)}, f32[1,32,16,384]{3,2,1,0:T(8,128)}) fusion(f32[1,32,16,384]{3,2,1,0:T(8,128)} %param.18, f32[32,16,384]{2,1,0:T(8,128)} %copy-done.4, f32[32,16,384]{2,1,0:T(8,128)S(1)} %multiply_add_fusion.1, f32[32,16,384]{2,1,0:T(8,128)S(1)} %fusion.169, f32[1,32,16,384]{3,2,1,0:T(8,128)S(1)} %copy-done.1, ...), kind=kLoop, calls=%fused_computation.298 | loop fusion | flops 2555904 | bytes 7864320 | tf_op jit(solution)/shard_map/add | solution.py:114
  110.3 0.0 all-reduce.6.cloned.1.call-update
  110.3 78.9 %all-reduce.6.cloned.1.call-done = f32[32,16,384]{2,1,0:T(8,128)} async-done(((f32[32,16,384]{2,1,0:T(8,128)}), f32[32,16,384]{2,1,0:T(8,128)}) %all-reduce.6.cloned.1.call-update) | async-done | bytes 786448 | tf_op jit(solution)/shard_map/psum | solution.py:114
  189.2 2.1 %copy.24 = f32[32,16,384]{2,1,0:T(8,128)} copy(f32[32,16,384]{2,1,0:T(8,128)} %all-reduce.6.cloned.1.call-done) | data formatting | bytes 1572864
  (23 shorter events, 0.1 us)
Async XLA Ops:
  7.2 17.4 %copy-start.14 = (s32[3]{0:T(128)S(1)}, s32[3]{0:T(128)}, u32[]{:S(2)}) copy-start(s32[3]{0:T(128)} %constant.78.clone.1) | copy-start | bytes 40
  7.2 20.1 %copy-start.12 = (s32[3]{0:T(128)S(1)}, s32[3]{0:T(128)}, u32[]{:S(2)}) copy-start(s32[3]{0:T(128)} %constant.108) | copy-start | bytes 40
  7.2 20.1 %copy-start.13 = (s32[3]{0:T(128)S(1)}, s32[3]{0:T(128)}, u32[]{:S(2)}) copy-start(s32[3]{0:T(128)} %constant.105) | copy-start | bytes 40
  7.2 20.9 %copy-start.1 = (f32[1,32,16,384]{3,2,1,0:T(8,128)S(1)}, f32[1,32,16,384]{3,2,1,0:T(8,128)}, u32[]{:S(2)}) copy-start(f32[1,32,16,384]{3,2,1,0:T(8,128)} %param.19) | copy-start | bytes 2359300
  7.2 15.4 %copy-start.11 = (f32[1,2]{1,0:T(1,128)S(1)}, f32[1,2]{1,0:T(1,128)}, u32[]{:S(2)}) copy-start(f32[1,2]{1,0:T(1,128)} %param.25) | copy-start | bytes 28
  7.2 19.3 %copy-start.7 = (f32[1,2,1024]{2,1,0:T(2,128)S(1)}, f32[1,2,1024]{2,1,0:T(2,128)}, u32[]{:S(2)}) copy-start(f32[1,2,1024]{2,1,0:T(2,128)} %param.29) | copy-start | bytes 24580
  7.2 19.9 %copy-start.5 = (s32[1,1024]{1,0:T(1,128)S(1)}, s32[1,1024]{1,0:T(1,128)}, u32[]{:S(2)}) copy-start(s32[1,1024]{1,0:T(1,128)} %param.26) | copy-start | bytes 12292
  7.2 19.9 %copy-start.9 = (s32[1,1024]{1,0:T(1,128)S(1)}, s32[1,1024]{1,0:T(1,128)}, u32[]{:S(2)}) copy-start(s32[1,1024]{1,0:T(1,128)} %param.28) | copy-start | bytes 12292
  7.3 19.9 %copy-start.8 = (s32[1,1024]{1,0:T(1,128)S(1)}, s32[1,1024]{1,0:T(1,128)}, u32[]{:S(2)}) copy-start(s32[1,1024]{1,0:T(1,128)} %param.27) | copy-start | bytes 12292
  7.3 181.9 %all-reduce.6.cloned.1.call-start = ((), (), s32[]{:S(2)}) async-start(), calls=%async_computation | async-start | bytes 1572864 | tf_op jit(solution)/shard_map/psum | solution.py:114
  9.0 30.9 %collective-permute-start.4 = (f32[4,16,384]{2,1,0:T(8,128)}, f32[4,16,384]{2,1,0:T(8,128)S(1)}, u32[]{:S(2)}, u32[]{:S(2)}) collective-permute-start(f32[4,16,384]{2,1,0:T(8,128)} %get-tuple-element.33), channel_id=1, source_target_pairs={{1,0},{2,1},{3,2},{5,4},{6,5},{7,6},{9,8},{10,9},{11,10},{13,12},{... | collective-permute-start | bytes 294920 | tf_op jit(solution)/shard_map/ppermute | solution.py:20
  10.3 29.6 %collective-permute-start.5 = (f32[4,16,384]{2,1,0:T(8,128)}, f32[4,16,384]{2,1,0:T(8,128)S(1)}, u32[]{:S(2)}, u32[]{:S(2)}) collective-permute-start(f32[4,16,384]{2,1,0:T(8,128)} %get-tuple-element.34), channel_id=1, source_target_pairs={{0,1},{1,2},{2,3},{4,5},{5,6},{6,7},{8,9},{9,10},{10,11},{12,13},{... | collective-permute-start | bytes 294920 | tf_op jit(solution)/shard_map/ppermute | solution.py:17
  14.3 13.8 %collective-permute-start = (f32[4,16,384]{2,1,0:T(8,128)S(1)}, f32[4,16,384]{2,1,0:T(8,128)S(1)}, u32[]{:S(2)}, u32[]{:S(2)}) collective-permute-start(f32[4,16,384]{2,1,0:T(8,128)S(1)} %get-tuple-element.37), channel_id=1, source_target_pairs={{1,0},{2,1},{3,2},{5,4},{6,5},{7,6},{9,8},{10,9},{11,10},{13,12},{... | collective-permute-start | bytes 294920 | tf_op jit(solution)/shard_map/ppermute | solution.py:20
  15.6 12.5 %collective-permute-start.1 = (f32[4,16,384]{2,1,0:T(8,128)S(1)}, f32[4,16,384]{2,1,0:T(8,128)S(1)}, u32[]{:S(2)}, u32[]{:S(2)}) collective-permute-start(f32[4,16,384]{2,1,0:T(8,128)S(1)} %get-tuple-element.38), channel_id=1, source_target_pairs={{0,1},{1,2},{2,3},{4,5},{5,6},{6,7},{8,9},{9,10},{10,11},{12,13},{... | collective-permute-start | bytes 294920 | tf_op jit(solution)/shard_map/ppermute | solution.py:17
  28.1 4.1 %copy-start.2 = (f32[32,16,384]{2,1,0:T(8,128)S(1)}, f32[32,16,384]{2,1,0:T(8,128)}, u32[]{:S(2)}) copy-start(f32[32,16,384]{2,1,0:T(8,128)} %param.17) | copy-start | bytes 2359300
  32.2 7.7 %copy-start.3 = (f32[1,32,16,384]{3,2,1,0:T(8,128)S(1)}, f32[1,32,16,384]{3,2,1,0:T(8,128)}, u32[]{:S(2)}) copy-start(f32[1,32,16,384]{3,2,1,0:T(8,128)} %param.21) | copy-start | bytes 2359300
  34.3 19.0 %collective-permute-start.2 = (f32[4,16,384]{2,1,0:T(8,128)}, f32[4,16,384]{2,1,0:T(8,128)S(1)}, u32[]{:S(2)}, u32[]{:S(2)}) collective-permute-start(f32[4,16,384]{2,1,0:T(8,128)} %get-tuple-element.35), channel_id=1, source_target_pairs={{1,0},{2,1},{3,2},{5,4},{6,5},{7,6},{9,8},{10,9},{11,10},{13,12},{... | collective-permute-start | bytes 294920 | tf_op jit(solution)/shard_map/ppermute | solution.py:20
  35.6 17.7 %collective-permute-start.3 = (f32[4,16,384]{2,1,0:T(8,128)}, f32[4,16,384]{2,1,0:T(8,128)S(1)}, u32[]{:S(2)}, u32[]{:S(2)}) collective-permute-start(f32[4,16,384]{2,1,0:T(8,128)} %get-tuple-element.36), channel_id=1, source_target_pairs={{0,1},{1,2},{2,3},{4,5},{5,6},{6,7},{8,9},{9,10},{10,11},{12,13},{... | collective-permute-start | bytes 294920 | tf_op jit(solution)/shard_map/ppermute | solution.py:17
  61.7 45.0 %copy-start = (f32[32,16,384]{2,1,0:T(8,128)}, f32[32,16,384]{2,1,0:T(8,128)S(1)}, u32[]{:S(2)}) copy-start(f32[32,16,384]{2,1,0:T(8,128)S(1)} %multiply_add_fusion.1) | copy-start | bytes 2359300
  61.7 18.2 %copy-start.6 = (f32[1,1,1024]{2,1,0:T(1,128)S(1)}, f32[1,1,1024]{2,1,0:T(1,128)}, u32[]{:S(2)}) copy-start(f32[1,1,1024]{2,1,0:T(1,128)} %get-tuple-element.40) | copy-start | bytes 12292
  61.7 18.2 %copy-start.10 = (pred[1024]{0:T(1024)(128)(4,1)S(1)}, pred[1024]{0:T(1024)(128)(4,1)}, u32[]{:S(2)}) copy-start(pred[1024]{0:T(1024)(128)(4,1)} %fusion.172) | copy-start | bytes 3076
  89.3 5.3 %copy-start.4 = (f32[32,16,384]{2,1,0:T(8,128)}, f32[32,16,384]{2,1,0:T(8,128)S(1)}, u32[]{:S(2)}) copy-start(f32[32,16,384]{2,1,0:T(8,128)S(1)} %fusion.168) | copy-start | bytes 2359300
  89.4 4.3 %collective-permute-start.6 = (f32[4,16,384]{2,1,0:T(8,128)S(1)}, f32[4,16,384]{2,1,0:T(8,128)S(1)}, u32[]{:S(2)}, u32[]{:S(2)}) collective-permute-start(f32[4,16,384]{2,1,0:T(8,128)S(1)} %get-tuple-element.31), channel_id=1, source_target_pairs={{1,0},{2,1},{3,2},{5,4},{6,5},{7,6},{9,8},{10,9},{11,10},{13,12},{... | collective-permute-start | bytes 294920 | tf_op jit(solution)/shard_map/ppermute | solution.py:20
  90.7 4.0 %collective-permute-start.7 = (f32[4,16,384]{2,1,0:T(8,128)S(1)}, f32[4,16,384]{2,1,0:T(8,128)S(1)}, u32[]{:S(2)}, u32[]{:S(2)}) collective-permute-start(f32[4,16,384]{2,1,0:T(8,128)S(1)} %get-tuple-element.32), channel_id=1, source_target_pairs={{0,1},{1,2},{2,3},{4,5},{5,6},{6,7},{8,9},{9,10},{10,11},{12,13},{... | collective-permute-start | bytes 294920 | tf_op jit(solution)/shard_map/ppermute | solution.py:17
Sparse Core Ops, SparseCore 0:
  110.5 78.6 all-reduce.5
where the time goes:
time: 199 us; the launch traced here: 198 us
  waiting for transfers between devices  79.8 us (40%)
  other arithmetic  35.3 us (18%)
  local copies, waits for them, and re-layouts  34.5 us (17%)
  starting transfers between devices  20.6 us (10%)
  between operations  20.4 us (10%)
  blocking collectives  7.5 us (4%)
    psum x1, waiting for transfers between devices, shards(): gradient = lax.psum(early_term + late_term, 'shot')  78.9 us
    gather x2, local copies, waits for them, and re-layouts, sample(): picked = field[local, ycells, zcells]  21.1 us
    ppermute x4, starting transfers between devices, with_halo(): lax.ppermute(lax.slice_in_dim(block, block.shape[dim] - width, None, axis...  15.4 us
    unnamed x5, other arithmetic  12.9 us
    add x4, other arithmetic, laplace_core(): total + weight * (padded[:, R:R + width_y, R + offset:R + offset + width_...  12.4 us
    psum x1, blocking collectives, shards(): traces = lax.psum(samples, 'dom')  7.5 us
    ppermute x4, starting transfers between devices, with_halo(): lax.ppermute(lax.slice_in_dim(block, 0, width, axis=dim), axis, backward)  5.14 us
    add x3, other arithmetic, advance(): 2.0 * current - before + coefficient * (laplace_core(extended) + sources)  5.01 us
  transfers between devices with their start and end apart: 9, of which 2 were waited for; matrix products, arithmetic and copies ran while one was open for 11% of the time, Pallas kernels for 0%

commit v1 on v0

v1 whole, which is shorter than its diff:
```python
import functools

import jax
import jax.numpy as jnp
import numpy as np
from jax import lax
from jax.experimental import pallas as pl
from jax.experimental.pallas import tpu as pltpu
from jax.sharding import PartitionSpec as P

R = 4
CH = 8
MESH = pl.DeviceIdType.MESH
SCALE = 5040.0
W0 = -3.0 * 14350.0
WK = (8064.0, -1008.0, 128.0, -9.0)
P1, Q3, P2, Q2 = range(4)


def band(size):
    out = np.zeros((size, size), np.float32)
    for k, weight in enumerate(WK, 1):
        out += weight * (np.eye(size, k=k) + np.eye(size, k=-k))
    return out


def kernel(
    dims,
    coef,
    older,
    recent,
    later,
    adj,
    srcs,
    amp,
    rcell,
    obs,
    zz,
    yy,
    out_p3,
    out_q1,
    out_g,
    p2,
    q2,
    cnt,
    o2,
    o3,
    grad,
    land,
    halo,
    hsend,
    hrecv,
    gsend,
    grecv,
):
    ndom, nshot = dims
    nx, ny, nz = coef.shape
    rows = CH * ny
    nch = nx // CH
    bits = nshot.bit_length() - 1
    parts = nch
    while parts > 1 and (nch * rows // parts) // nshot < 8:
        parts //= 2
    prow = nch * rows // parts

    dom = lax.axis_index("dom")
    shot = lax.axis_index("shot")
    has_lo = dom > 0
    has_hi = dom < ndom - 1
    bit = [(shot // (1 << b)) % 2 for b in range(bits)]
    partner = [shot + (1 << b) * (1 - 2 * bit[b]) for b in range(bits)]

    barrier = pltpu.get_barrier_semaphore()
    for b in range(bits):
        pl.semaphore_signal(barrier, inc=1, device_id={"shot": partner[b]}, device_id_type=MESH)

    @pl.when(has_lo)
    def _():
        pl.semaphore_signal(barrier, inc=1, device_id={"dom": dom - 1}, device_id_type=MESH)

    @pl.when(has_hi)
    def _():
        pl.semaphore_signal(barrier, inc=1, device_id={"dom": dom + 1}, device_id_type=MESH)

    pl.semaphore_wait(barrier, bits + has_lo.astype(jnp.int32) + has_hi.astype(jnp.int32))

    def down(f, ref):
        return pltpu.make_async_remote_copy(
            src_ref=ref.at[pl.ds(0, R)],
            dst_ref=halo.at[f, 1],
            send_sem=hsend.at[f, 0],
            recv_sem=hrecv.at[f, 1],
            device_id={"dom": dom - 1},
            device_id_type=MESH,
        )

    def up(f, ref):
        return pltpu.make_async_remote_copy(
            src_ref=ref.at[pl.ds(nx - R, R)],
            dst_ref=halo.at[f, 0],
            send_sem=hsend.at[f, 1],
            recv_sem=hrecv.at[f, 0],
            device_id={"dom": dom + 1},
            device_id_type=MESH,
        )

    def send_lo(f, ref):
        @pl.when(has_lo)
        def _():
            down(f, ref).start()

    def send_hi(f, ref):
        @pl.when(has_hi)
        def _():
            up(f, ref).start()

    def recv_lo(f, ref):
        @pl.when(has_lo)
        def _():
            up(f, ref).wait_recv()

    def recv_hi(f, ref):
        @pl.when(has_hi)
        def _():
            down(f, ref).wait_recv()

    def sent(f, ref):
        @pl.when(has_lo)
        def _():
            down(f, ref).wait_send()

        @pl.when(has_hi)
        def _():
            up(f, ref).wait_send()

    send_lo(P1, recent)
    send_hi(P1, recent)
    send_lo(Q3, adj)
    send_hi(Q3, adj)

    edge = jnp.zeros((R, ny, nz), jnp.float32)

    @pl.when(dom == 0)
    def _():
        for f in range(4):
            halo[f, 0] = edge

    @pl.when(dom == ndom - 1)
    def _():
        for f in range(4):
            halo[f, 1] = edge

    base = dom * nx
    rowid = (rcell[0:1, :] - base) * ny + rcell[1:2, :]
    zid = rcell[2:3, :]
    nrecv = rowid.shape[1]
    pick = (lax.broadcasted_iota(jnp.int32, (nx * ny, nrecv), 0) == rowid).astype(jnp.float32).astype(jnp.bfloat16)
    onz = lax.broadcasted_iota(jnp.int32, (nz, nrecv), 0) == zid
    nt = (((1,), (1,)), ((), ()))

    def spread(values):
        side = jnp.where(onz, values, 0.0).astype(jnp.bfloat16)
        return lax.dot_general(pick, side, nt, preferred_element_type=jnp.float32)

    cnt[...] = spread(1.0)
    for ref, t in ((o3, 1), (o2, 0)):
        value = obs[t : t + 1, :]
        high = value.astype(jnp.bfloat16).astype(jnp.float32)
        ref[...] = spread(high)
        ref[...] += spread(value - high)

    def window(ref, f, c):
        low = ref[c * CH - R : c * CH] if c > 0 else halo[f, 0]
        high = ref[(c + 1) * CH : (c + 1) * CH + R] if c < nch - 1 else halo[f, 1]
        return jnp.concatenate([low, ref[c * CH : (c + 1) * CH], high], axis=0)

    def laplace(ref, f, c):
        ext = window(ref, f, c)
        center = ext[R : R + CH]
        total = W0 * center
        for k, weight in enumerate(WK, 1):
            total = total + weight * (ext[R + k : R + k + CH] + ext[R - k : R - k + CH])
        flat = center.reshape(rows, nz)
        high = flat.astype(jnp.bfloat16)
        low = (flat - high.astype(jnp.float32)).astype(jnp.bfloat16)
        along_z = jnp.dot(jnp.concatenate([high, low], axis=1), zz[...], preferred_element_type=jnp.float32)
        along_y = jnp.dot(yy[...], jnp.concatenate([high, low], axis=0), preferred_element_type=jnp.float32)
        return (total.reshape(rows, nz) + (along_z + along_y)) * (1.0 / SCALE)

    def flat(ref, c):
        return ref[c * CH : (c + 1) * CH].reshape(rows, nz)

    def put(ref, c, value):
        ref[c * CH : (c + 1) * CH] = value.reshape(CH, ny, nz)

    srow = (srcs[0, 0] - base) * ny + srcs[1, 0]
    szed = srcs[2, 0]

    def source(c, t):
        row = lax.broadcasted_iota(jnp.int32, (rows, nz), 0) + c * rows
        lane = lax.broadcasted_iota(jnp.int32, (rows, nz), 1)
        return jnp.where((row == srow) & (lane == szed), amp[0, t], 0.0)

    def at(ref, c):
        return ref[c * rows : (c + 1) * rows, :]

    def step_p2(c):
        value = 2.0 * flat(recent, c) - flat(older, c) + flat(coef, c) * (laplace(recent, P1, c) + source(c, 0))
        put(p2, c, value)

    def step_p3(c):
        value = 2.0 * flat(p2, c) - flat(recent, c) + flat(coef, c) * (laplace(p2, P2, c) + source(c, 1))
        put(out_p3, c, value)

    def step_q2(c):
        points = at(cnt, c) * flat(out_p3, c) - at(o3, c)
        value = 2.0 * flat(adj, c) - flat(later, c) + flat(coef, c) * (laplace(adj, Q3, c) + points)
        put(q2, c, value)

    def step_q1(c):
        two = flat(p2, c)
        points = at(cnt, c) * two - at(o2, c)
        now = flat(q2, c)
        value = 2.0 * now - flat(adj, c) + flat(coef, c) * (laplace(q2, Q2, c) + points)
        put(out_q1, c, value)
        one = flat(recent, c)
        early = two - 2.0 * one + flat(older, c)
        late = flat(out_p3, c) - 2.0 * two + one
        grad[c * rows : (c + 1) * rows, :] = value * early + now * late

    def exchange(p, order):
        off = p * prow
        length = prow
        slot = 0
        pending = []
        for t, b in enumerate(order):
            length //= 2
            keep = pl.multiple_of(off + bit[b] * length, 8)
            give = pl.multiple_of(off + (1 - bit[b]) * length, 8)
            copy = pltpu.make_async_remote_copy(
                src_ref=grad.at[pl.ds(give, length)],
                dst_ref=land.at[pl.ds(p * prow + slot, length)],
                send_sem=gsend.at[p, t],
                recv_sem=grecv.at[p, t],
                device_id={"shot": partner[b]},
                device_id_type=MESH,
            )
            copy.start()
            pending.append(copy)
            yield
            copy.wait_recv()
            total = grad[pl.ds(keep, length), :] + land[p * prow + slot : p * prow + slot + length, :]
            if t < len(order) - 1:
                grad[pl.ds(keep, length), :] = total
            else:
                out_g[pl.ds(keep, length), :] = total
            off = keep
            slot += length
        for t, b in enumerate(reversed(order)):
            copy = pltpu.make_async_remote_copy(
                src_ref=out_g.at[pl.ds(off, length)],
                dst_ref=out_g.at[pl.ds(off, length)],
                send_sem=gsend.at[p, bits + t],
                recv_sem=grecv.at[p, bits + t],
                device_id={"shot": partner[b]},
                device_id_type=MESH,
            )
            copy.start()
            pending.append(copy)
            yield
            copy.wait_recv()
            off = pl.multiple_of(off - bit[b] * length, 8)
            length *= 2
        for copy in pending:
            copy.wait_send()

    edges = (0, nch - 1)
    inner = tuple(range(1, nch - 1))
    per = nch // parts
    ready = set()
    running = []

    def advance():
        for run in list(running):
            if next(run, True):
                running.remove(run)

    def finish(c):
        step_q1(c)
        ready.add(c)
        p = c // per
        if all(i in ready for i in range(p * per, (p + 1) * per)):
            order = list(range(bits))
            if p % 2 and bits > 1:
                order[0], order[1] = order[1], order[0]
            run = exchange(p, order)
            next(run, None)
            running.append(run)

    for c in inner:
        step_p2(c)
    recv_lo(P1, recent)
    step_p2(0)
    send_lo(P2, p2)
    recv_hi(P1, recent)
    step_p2(nch - 1)
    send_hi(P2, p2)
    for c in inner:
        step_p3(c)
        step_q2(c)
    recv_lo(Q3, adj)
    recv_lo(P2, p2)
    step_p3(0)
    step_q2(0)
    send_lo(Q2, q2)
    recv_hi(Q3, adj)
    recv_hi(P2, p2)
    step_p3(nch - 1)
    step_q2(nch - 1)
    send_hi(Q2, q2)
    for c in inner:
        finish(c)
    recv_lo(Q2, q2)
    finish(0)
    recv_hi(Q2, q2)
    finish(nch - 1)
    while running:
        advance()
    sent(P1, recent)
    sent(Q3, adj)
    sent(P2, p2)
    sent(Q2, q2)


def shards(
    coefficient,
    fwd_older,
    fwd_recent,
    adj_later,
    adj_recent,
    source_xcell,
    source_ycell,
    source_zcell,
    amplitude,
    receiver_xcell,
    receiver_ycell,
    receiver_zcell,
    observed,
):
    ndom, nshot = lax.axis_size("dom"), lax.axis_size("shot")
    nx, ny, nz = coefficient.shape
    cells = nx * ny
    bits = nshot.bit_length() - 1
    zmat = band(nz)
    ymat = np.kron(np.eye(CH), band(ny))
    zz = jnp.asarray(np.concatenate([zmat, zmat], 0), jnp.bfloat16)
    yy = jnp.asarray(np.concatenate([ymat, ymat], 1), jnp.bfloat16)
    srcs = jnp.stack([source_xcell, source_ycell, source_zcell])
    rcell = jnp.concatenate([receiver_xcell, receiver_ycell, receiver_zcell])
    field = jax.ShapeDtypeStruct((nx, ny, nz), jnp.float32)
    vmem = pl.BlockSpec(memory_space=pltpu.VMEM)
    smem = pl.BlockSpec(memory_space=pltpu.SMEM)
    block = pltpu.VMEM((nx, ny, nz), jnp.float32)
    plane = pltpu.VMEM((cells, nz), jnp.float32)
    p3, q1, grad = pl.pallas_call(
        functools.partial(kernel, (ndom, nshot)),
        out_shape=(field, field, jax.ShapeDtypeStruct((cells, nz), jnp.float32)),
        in_specs=[vmem] * 5 + [smem] * 2 + [vmem] * 4,
        out_specs=(vmem,) * 3,
        scratch_shapes=[
            block,
            block,
            plane,
            plane,
            plane,
            plane,
            plane,
            pltpu.VMEM((4, 2, R, ny, nz), jnp.float32),
            pltpu.SemaphoreType.DMA((4, 2)),
            pltpu.SemaphoreType.DMA((4, 2)),
            pltpu.SemaphoreType.DMA((nx // CH, 2 * bits)),
            pltpu.SemaphoreType.DMA((nx // CH, 2 * bits)),
        ],
        compiler_params=pltpu.CompilerParams(
            collective_id=0, has_side_effects=True, vmem_limit_bytes=48 * 1024 * 1024
        ),
        cost_estimate=pl.CostEstimate(flops=4 * 10**9, bytes_accessed=8 * 4 * cells * nz, transcendentals=0),
        name="wave_steps",
    )(
        coefficient,
        fwd_older[0],
        fwd_recent[0],
        adj_later[0],
        adj_recent[0],
        srcs,
        amplitude,
        rcell,
        observed[0],
        zz,
        yy,
    )
    return p3[None], q1[None], grad.reshape(nx, ny, nz)


def solution(mesh):
    return jax.shard_map(
        shards,
        mesh=mesh,
        in_specs=(
            P("dom", None, None),
            P("shot", "dom", None, None),
            P("shot", "dom", None, None),
            P("shot", "dom", None, None),
            P("shot", "dom", None, None),
            P("shot"),
            P("shot"),
            P("shot"),
            P("shot", None),
            P("shot", None),
            P("shot", None),
            P("shot", None),
            P("shot", None, None),
        ),
        out_specs=(
            P("shot", "dom", None, None),
            P("shot", "dom", None, None),
            P("dom", None, None),
        ),
        check_vma=False,
    )
```

time: 199 us -> 52.4 us (0.26)
  waiting for transfers between devices: 79.8 us -> 0 us
  Pallas kernels: 0 us -> 38.3 us
  other arithmetic: 35.3 us -> 0.09 us
  local copies, waits for them, and re-layouts: 34.5 us -> 10.5 us
  starting transfers between devices: 20.6 us -> 0 us
  between operations: 20.4 us -> 2.6 us
  blocking collectives: 7.5 us -> 0 us
    psum x1 -> x0, waiting for transfers between devices: 78.9 us -> none  [shards(): gradient = lax.psum(early_term + late_term, 'shot')]
    pallas_call x0 -> x1, Pallas kernels: none -> 38.3 us  [shards(): pl.pallas_call(functools.partial(kernel, (ndom, nshot)), out_shape=(field...]
    gather x2 -> x0, local copies, waits for them, and re-layouts: 21.1 us -> none  [sample(): picked = field[local, ycells, zcells]]
    add x8 -> x0, other arithmetic: 21 us -> none  [the longest x4 12.4 us: laplace_core(): total + weight * (padded[:, R:R + width_y, R + offset:R + offset + width_...]
    ppermute x8 -> x0, starting transfers between devices: 20.6 us -> none  [the longest x4 15.4 us: with_halo(): lax.ppermute(lax.slice_in_dim(block, block.shape[dim] - width, None, axis...]
    unnamed x5 -> x0, other arithmetic: 12.9 us -> none
    psum x1 -> x0, blocking collectives: 7.5 us -> none  [shards(): traces = lax.psum(samples, 'dom')]
    unnamed x33 -> x25, local copies, waits for them, and re-layouts: 3.38 us -> 10.4 us
  transfers between devices with their start and end apart: 9 -> 0, of which waited for: 2 -> 0; matrix products, arithmetic and copies ran while one was open for 11% -> 0% of each run, Pallas kernels for 0% -> 0%
where the time goes in v1:
time: 52.4 us; the launch traced here: 51.5 us
  Pallas kernels  38.3 us (73%)
  local copies, waits for them, and re-layouts  10.5 us (20%)
  between operations  2.6 us (5%)
    pallas_call x1, Pallas kernels, shards(): pl.pallas_call(functools.partial(kernel, (ndom, nshot)), out_shape=(field...  38.3 us
    unnamed x25, local copies, waits for them, and re-layouts  10.4 us

profile of v1, /device:TPU:0, one launch (start us, length us, event | category | flops | bytes accessed | tf_op | source)
XLA Modules:
  0.0 51.5 jit_solution(9013175034106562035)
XLA Ops:
  2.6 0.0 copy-start.10
  2.6 0.1 pad_add_fusion.1
  2.7 0.0 copy-start.8
  2.7 0.0 copy-start.9
  2.7 0.1 copy.18.srcs
  2.7 0.5 copy-done.10
  3.3 0.1 copy-done.8
  3.3 0.0 copy-done.9
  3.4 0.0 copy-start.4
  3.4 0.0 copy-start.5
  3.4 0.7 %copy-done.4 = f32[1,2,1024]{2,1,0:T(2,128)S(1)} copy-done((f32[1,2,1024]{2,1,0:T(2,128)S(1)}, f32[1,2,1024]{2,1,0:T(2,128)}, u32[]{:S(2)}) %copy-start.4) | copy-done | bytes 8216
  4.1 0.0 copy-done.5
  4.1 0.0 copy-start
  4.1 1.1 %copy-done = f32[32,16,384]{2,1,0:T(8,128)S(1)} copy-done((f32[32,16,384]{2,1,0:T(8,128)S(1)}, f32[32,16,384]{2,1,0:T(8,128)}, u32[]{:S(2)}) %copy-start) | copy-done | bytes 786456
  5.2 0.0 copy-start.1
  5.2 1.1 %copy-done.1 = f32[1,32,16,384]{3,2,1,0:T(8,128)S(1)} copy-done((f32[1,32,16,384]{3,2,1,0:T(8,128)S(1)}, f32[1,32,16,384]{3,2,1,0:T(8,128)}, u32[]{:S(2)}) %copy-start.1) | copy-done | bytes 786456
  6.3 0.0 copy-start.2
  6.3 1.1 %copy-done.2 = f32[1,32,16,384]{3,2,1,0:T(8,128)S(1)} copy-done((f32[1,32,16,384]{3,2,1,0:T(8,128)S(1)}, f32[1,32,16,384]{3,2,1,0:T(8,128)}, u32[]{:S(2)}) %copy-start.2) | copy-done | bytes 786456
  7.5 0.0 copy-start.3
  7.5 1.1 %copy-done.3 = f32[1,32,16,384]{3,2,1,0:T(8,128)S(1)} copy-done((f32[1,32,16,384]{3,2,1,0:T(8,128)S(1)}, f32[1,32,16,384]{3,2,1,0:T(8,128)}, u32[]{:S(2)}) %copy-start.3) | copy-done | bytes 786456
  8.6 0.0 copy-start.6
  8.6 1.1 %copy-done.6 = bf16[768,384]{1,0:T(8,128)(2,1)S(1)} copy-done((bf16[768,384]{1,0:T(8,128)(2,1)S(1)}, bf16[768,384]{1,0:T(8,128)(2,1)}, u32[]{:S(2)}) %copy-start.6) | copy-done | bytes 589848
  9.7 0.0 copy-start.7
  9.7 0.8 %copy-done.7 = bf16[128,256]{1,0:T(8,128)(2,1)S(1)} copy-done((bf16[128,256]{1,0:T(8,128)(2,1)S(1)}, bf16[128,256]{1,0:T(8,128)(2,1)}, u32[]{:S(2)}) %copy-start.7) | copy-done | bytes 65560
  10.5 38.3 %wave_steps.1 = (f32[32,16,384]{2,1,0:T(8,128)S(1)}, f32[32,16,384]{2,1,0:T(8,128)S(1)}, f32[512,384]{1,0:T(8,128)S(1)}) custom-call(f32[32,16,384]{2,1,0:T(8,128)S(1)} %copy-done, f32[32,16,384]{2,1,0:T(8,128)S(1)} %bitcast.17, f32[32,16,384]{2,1,0:T(8,128)S(1)} %bitcast.18, f32[32,16,384]{2,1,0:T(8,128)S(1)} %bitcast.19, f32[32,16,384]{2,1,0:T(8,128)} %bitcast.21, ...), custom_call_target="tpu_custom_call" | custom-call | flops 4000000000 | bytes 6291456 | tf_op jit(solution)/shard_map/wave_steps/pallas_call | solution.py:365
  48.8 0.9 %copy.25 = f32[1,32,16,384]{3,2,1,0:T(8,128)} copy(f32[1,32,16,384]{3,2,1,0:T(8,128)S(1)} %bitcast.16) | data formatting | bytes 1572864
  49.7 0.9 %copy.26 = f32[1,32,16,384]{3,2,1,0:T(8,128)} copy(f32[1,32,16,384]{3,2,1,0:T(8,128)S(1)} %bitcast.15) | data formatting | bytes 1572864
  50.6 0.9 %copy.27 = f32[32,16,384]{2,1,0:T(8,128)} copy(f32[32,16,384]{2,1,0:T(8,128)S(1)} %bitcast.14) | data formatting | bytes 1572864
  (1 shorter events, 0.0 us)
Async XLA Ops:
  2.6 0.7 %copy-start.10 = (s32[1,1024]{1,0:T(1,128)S(1)}, s32[1,1024]{1,0:T(1,128)}, u32[]{:S(2)}) copy-start(s32[1,1024]{1,0:T(1,128)} %param.24) | copy-start | bytes 12292
  2.7 0.7 %copy-start.8 = (s32[1,1024]{1,0:T(1,128)S(1)}, s32[1,1024]{1,0:T(1,128)}, u32[]{:S(2)}) copy-start(s32[1,1024]{1,0:T(1,128)} %param.26) | copy-start | bytes 12292
  2.7 0.7 %copy-start.9 = (s32[1,1024]{1,0:T(1,128)S(1)}, s32[1,1024]{1,0:T(1,128)}, u32[]{:S(2)}) copy-start(s32[1,1024]{1,0:T(1,128)} %param.25) | copy-start | bytes 12292
  3.4 0.7 %copy-start.4 = (f32[1,2,1024]{2,1,0:T(2,128)S(1)}, f32[1,2,1024]{2,1,0:T(2,128)}, u32[]{:S(2)}) copy-start(f32[1,2,1024]{2,1,0:T(2,128)} %param.27) | copy-start | bytes 24580
  3.4 0.7 %copy-start.5 = (f32[1,2]{1,0:T(1,128)S(1)}, f32[1,2]{1,0:T(1,128)}, u32[]{:S(2)}) copy-start(f32[1,2]{1,0:T(1,128)} %amp.1) | copy-start | bytes 28
  4.1 1.1 %copy-start = (f32[32,16,384]{2,1,0:T(8,128)S(1)}, f32[32,16,384]{2,1,0:T(8,128)}, u32[]{:S(2)}) copy-start(f32[32,16,384]{2,1,0:T(8,128)} %coef.1) | copy-start | bytes 2359300
  5.2 1.1 %copy-start.1 = (f32[1,32,16,384]{3,2,1,0:T(8,128)S(1)}, f32[1,32,16,384]{3,2,1,0:T(8,128)}, u32[]{:S(2)}) copy-start(f32[1,32,16,384]{3,2,1,0:T(8,128)} %param.16) | copy-start | bytes 2359300
  6.3 1.1 %copy-start.2 = (f32[1,32,16,384]{3,2,1,0:T(8,128)S(1)}, f32[1,32,16,384]{3,2,1,0:T(8,128)}, u32[]{:S(2)}) copy-start(f32[1,32,16,384]{3,2,1,0:T(8,128)} %param.17) | copy-start | bytes 2359300
  7.5 1.1 %copy-start.3 = (f32[1,32,16,384]{3,2,1,0:T(8,128)S(1)}, f32[1,32,16,384]{3,2,1,0:T(8,128)}, u32[]{:S(2)}) copy-start(f32[1,32,16,384]{3,2,1,0:T(8,128)} %param.18) | copy-start | bytes 2359300
  8.6 1.1 %copy-start.6 = (bf16[768,384]{1,0:T(8,128)(2,1)S(1)}, bf16[768,384]{1,0:T(8,128)(2,1)}, u32[]{:S(2)}) copy-start(bf16[768,384]{1,0:T(8,128)(2,1)} %constant.4.clone.zz) | copy-start | bytes 1769476
  9.7 0.8 %copy-start.7 = (bf16[128,256]{1,0:T(8,128)(2,1)S(1)}, bf16[128,256]{1,0:T(8,128)(2,1)}, u32[]{:S(2)}) copy-start(bf16[128,256]{1,0:T(8,128)(2,1)} %constant.5.clone.yy) | copy-start | bytes 196612

commit v2 on v0

v2 whole, which is shorter than its diff:
```python
import functools

import jax
import jax.numpy as jnp
from jax import lax
from jax.experimental import pallas as pl
from jax.experimental.pallas import tpu as pltpu
from jax.sharding import PartitionSpec as P

R = 4
CH = 8
MESH = pl.DeviceIdType.MESH
SCALE = 5040.0
W0 = -3.0 * 14350.0
WK = (8064.0, -1008.0, 128.0, -9.0)
P1, Q3, P2, Q2 = range(4)


def band(size, group):
    row = lax.broadcasted_iota(jnp.int32, (size, size), 0)
    col = lax.broadcasted_iota(jnp.int32, (size, size), 1)
    apart = jnp.abs(row - col)
    out = jnp.zeros((size, size), jnp.float32)
    for k, weight in enumerate(WK, 1):
        out = jnp.where(apart == k, weight, out)
    if group < size:
        out = jnp.where(row // group == col // group, out, 0.0)
    return out.astype(jnp.bfloat16)


def kernel(
    dims,
    coef_in,
    older_in,
    recent_in,
    later_in,
    adj_in,
    sx,
    sy,
    sz,
    amp,
    rx,
    ry,
    rz,
    obs,
    out_p3,
    out_q1,
    out_g,
    p3,
    q1,
    gsum,
    coef,
    older,
    later,
    p1,
    q3,
    p2,
    q2,
    zz,
    yy,
    cnt,
    o2,
    o3,
    grad,
    land,
    load,
    save,
    hsend,
    hrecv,
    gsend,
    grecv,
):
    ndom, nshot = dims
    nx, ny, nz = coef.shape
    rows = CH * ny
    nch = nx // CH
    bits = nshot.bit_length() - 1
    parts = gsend.shape[0]
    prow = nx * ny // parts

    dom = lax.axis_index("dom")
    shot = lax.axis_index("shot")
    has_lo = dom > 0
    has_hi = dom < ndom - 1
    bit = [(shot // (1 << b)) % 2 for b in range(bits)]
    partner = [shot + (1 << b) * (1 - 2 * bit[b]) for b in range(bits)]

    own = pl.ds(R, nx)
    loads = [
        pltpu.make_async_copy(src, dst, load.at[i])
        for i, (src, dst) in enumerate(
            (
                (recent_in, p1.at[own]),
                (older_in, older),
                (coef_in, coef),
                (adj_in, q3.at[own]),
                (later_in, later),
            )
        )
    ]
    for copy in loads:
        copy.start()

    barrier = pltpu.get_barrier_semaphore()
    for b in range(bits):
        pl.semaphore_signal(barrier, inc=1, device_id={"shot": partner[b]}, device_id_type=MESH)

    @pl.when(has_lo)
    def _():
        pl.semaphore_signal(barrier, inc=1, device_id={"dom": dom - 1}, device_id_type=MESH)

    @pl.when(has_hi)
    def _():
        pl.semaphore_signal(barrier, inc=1, device_id={"dom": dom + 1}, device_id_type=MESH)

    pl.semaphore_wait(barrier, bits + has_lo.astype(jnp.int32) + has_hi.astype(jnp.int32))

    def down(f, src, first, ref):
        return pltpu.make_async_remote_copy(
            src_ref=src.at[pl.ds(first, R)],
            dst_ref=ref.at[pl.ds(R + nx, R)],
            send_sem=hsend.at[f, 0],
            recv_sem=hrecv.at[f, 1],
            device_id={"dom": dom - 1},
            device_id_type=MESH,
        )

    def up(f, src, first, ref):
        return pltpu.make_async_remote_copy(
            src_ref=src.at[pl.ds(first + nx - R, R)],
            dst_ref=ref.at[pl.ds(0, R)],
            send_sem=hsend.at[f, 1],
            recv_sem=hrecv.at[f, 0],
            device_id={"dom": dom + 1},
            device_id_type=MESH,
        )

    def both(act, f, src, first, ref):
        @pl.when(has_lo)
        def _():
            act(down, up, f, src, first, ref)

        @pl.when(has_hi)
        def _():
            act(up, down, f, src, first, ref)

    def send(*args):
        both(lambda mine, other, *rest: mine(*rest).start(), *args)

    def receive(*args):
        both(lambda mine, other, *rest: other(*rest).wait_recv(), *args)

    def sent(*args):
        both(lambda mine, other, *rest: mine(*rest).wait_send(), *args)

    halo_p1 = (P1, recent_in, 0, p1)
    halo_q3 = (Q3, adj_in, 0, q3)
    halo_p2 = (P2, p2, R, p2)
    halo_q2 = (Q2, q2, R, q2)
    send(*halo_p1)
    send(*halo_q3)

    zmat = band(nz, nz)
    zz[0:nz, :] = zmat
    zz[nz : 2 * nz, :] = zmat
    ymat = band(rows, ny)
    yy[:, 0:rows] = ymat
    yy[:, rows : 2 * rows] = ymat

    nothing = jnp.zeros((R, ny, nz), jnp.float32)

    @pl.when(dom == 0)
    def _():
        for ref in (p1, q3, p2, q2):
            ref[0:R] = nothing

    @pl.when(dom == ndom - 1)
    def _():
        for ref in (p1, q3, p2, q2):
            ref[R + nx : R + nx + R] = nothing

    base = dom * nx
    nrecv = rx.shape[1]
    rowid = (rx[...] - base) * ny + ry[...]
    pick = (lax.broadcasted_iota(jnp.int32, (nx * ny, nrecv), 0) == rowid).astype(jnp.float32).astype(jnp.bfloat16)
    onz = lax.broadcasted_iota(jnp.int32, (nz, nrecv), 0) == rz[...]
    nt = (((1,), (1,)), ((), ()))

    def spread(values):
        side = jnp.where(onz, values, 0.0).astype(jnp.bfloat16)
        return lax.dot_general(pick, side, nt, preferred_element_type=jnp.float32)

    def observe(t):
        value = obs[t : t + 1, :]
        high = value.astype(jnp.bfloat16).astype(jnp.float32)
        return spread(high) + spread(value - high)

    def laplace(ref, c):
        ext = ref[pl.ds(c * CH, CH + 2 * R)]
        center = ext[R : R + CH]
        total = W0 * center
        for k, weight in enumerate(WK, 1):
            total = total + weight * (ext[R + k : R + k + CH] + ext[R - k : R - k + CH])
        flat = center.reshape(rows, nz)
        high = flat.astype(jnp.bfloat16)
        low = (flat - high.astype(jnp.float32)).astype(jnp.bfloat16)
        along_z = jnp.dot(jnp.concatenate([high, low], axis=1), zz[...], preferred_element_type=jnp.float32)
        along_y = jnp.dot(yy[...], jnp.concatenate([high, low], axis=0), preferred_element_type=jnp.float32)
        return (total.reshape(rows, nz) + (along_z + along_y)) * (1.0 / SCALE)

    def flat(ref, c, first=0):
        return ref[pl.ds(first + c * CH, CH)].reshape(rows, nz)

    def put(ref, c, value, first=0):
        ref[pl.ds(first + c * CH, CH)] = value.reshape(CH, ny, nz)

    def at(c):
        return pl.ds(pl.multiple_of(c * rows, rows), rows)

    srow = (sx[0] - base) * ny + sy[0]
    szed = sz[0]

    def source(c, t):
        row = lax.broadcasted_iota(jnp.int32, (rows, 1), 0) + c * rows
        lane = lax.broadcasted_iota(jnp.int32, (1, nz), 1)
        return jnp.where(row == srow, amp[0, t], 0.0) * jnp.where(lane == szed, 1.0, 0.0)

    def step_p2(c):
        value = 2.0 * flat(p1, c, R) - flat(older, c) + flat(coef, c) * (laplace(p1, c) + source(c, 0))
        put(p2, c, value, R)

    def step_p3(c):
        value = 2.0 * flat(p2, c, R) - flat(p1, c, R) + flat(coef, c) * (laplace(p2, c) + source(c, 1))
        put(p3, c, value)

    def step_q2(c):
        points = cnt[at(c), :] * flat(p3, c) - o3[at(c), :]
        value = 2.0 * flat(q3, c, R) - flat(later, c) + flat(coef, c) * (laplace(q3, c) + points)
        put(q2, c, value, R)

    def step_q1(c):
        two = flat(p2, c, R)
        points = cnt[at(c), :] * two - o2[at(c), :]
        now = flat(q2, c, R)
        value = 2.0 * now - flat(q3, c, R) + flat(coef, c) * (laplace(q2, c) + points)
        put(q1, c, value)
        one = flat(p1, c, R)
        early = two - 2.0 * one + flat(older, c)
        late = flat(p3, c) - 2.0 * two + one
        grad[at(c), :] = value * early + now * late

    def sweep(before_edges, body):
        def turn(i, carry):
            @pl.when(i == nch - 2)
            def _():
                before_edges()

            body(lax.rem(i + 1, nch))
            return carry

        lax.fori_loop(0, nch, turn, 0)

    def order_of(h):
        order = list(range(bits))
        if h and bits > 1:
            order[0], order[1] = order[1], order[0]
        return order

    def place(p, h, t):
        off = p * prow
        for u, b in enumerate(order_of(h)[:t]):
            off = off + bit[b] * (prow >> (u + 1))
        return off

    def rows_at(off, length):
        return pl.ds(pl.multiple_of(off, 8), length)

    def slot(p, t):
        return rows_at(p * prow + prow - (prow >> t), prow >> (t + 1))

    def reduce_copy(p, h, t):
        b = order_of(h)[t]
        length = prow >> (t + 1)
        give = place(p, h, t) + (1 - bit[b]) * length
        return pltpu.make_async_remote_copy(
            src_ref=grad.at[rows_at(give, length)],
            dst_ref=land.at[slot(p, t)],
            send_sem=gsend.at[p, t],
            recv_sem=grecv.at[p, t],
            device_id={"shot": partner[b]},
            device_id_type=MESH,
        )

    def gather_copy(p, h, t):
        rows_held = rows_at(place(p, h, t + 1), prow >> (t + 1))
        return pltpu.make_async_remote_copy(
            src_ref=gsum.at[rows_held],
            dst_ref=gsum.at[rows_held],
            send_sem=gsend.at[p, bits + t],
            recv_sem=grecv.at[p, bits + t],
            device_id={"shot": partner[order_of(h)[t]]},
            device_id_type=MESH,
        )

    def save_sum(p):
        return pltpu.make_async_copy(gsum.at[rows_at(p * prow, prow)], out_g.at[rows_at(p * prow, prow)], save.at[2 + p])

    def advance(p, h, n):
        if n < bits:
            reduce_copy(p, h, n).wait_recv()
            keep = rows_at(place(p, h, n + 1), prow >> (n + 1))
            total = grad[keep, :] + land[slot(p, n), :]
            if n < bits - 1:
                grad[keep, :] = total
                reduce_copy(p, h, n + 1).start()
            else:
                gsum[keep, :] = total
                gather_copy(p, h, bits - 1).start()
        else:
            t = 2 * bits - 1 - n
            gather_copy(p, h, t).wait_recv()
            if t:
                gather_copy(p, h, t - 1).start()
            else:
                save_sum(p).start()

    cnt[...] = spread(1.0)
    o3[...] = observe(1)
    for copy in loads[:3]:
        copy.wait()
    sweep(lambda: receive(*halo_p1), step_p2)
    send(*halo_p2)
    o2[...] = observe(0)
    for copy in loads[3:]:
        copy.wait()

    def middle(c):
        step_p3(c)
        step_q2(c)

    def arrive():
        receive(*halo_q3)
        receive(*halo_p2)

    sweep(arrive, middle)
    send(*halo_q2)
    save_p3 = pltpu.make_async_copy(p3, out_p3, save.at[0])
    save_q1 = pltpu.make_async_copy(q1, out_q1, save.at[1])
    save_p3.start()
    per = max(parts // nch, 1)

    def last(c):
        step_q1(c)
        if parts >= nch:
            for h in range(per):
                reduce_copy(c * per + h, h % 2, 0).start()

    sweep(lambda: receive(*halo_q2), last)
    save_q1.start()
    if parts < nch:
        for p in range(parts):
            reduce_copy(p, p % 2, 0).start()
    groups = [[(((c + 1) % nch) * per + h, h % 2) for h in range(per)] for c in range(nch)]
    if parts < nch:
        groups = [[(p, p % 2)] for p in range(parts)]
    steps = 2 * bits
    for turn in range(steps + len(groups) - 1):
        for g, group in enumerate(groups):
            if 0 <= turn - g < steps:
                for p, h in group:
                    advance(p, h, turn - g)
    for p in range(parts):
        h = (p % per) % 2 if parts >= nch else p % 2
        for t in range(bits):
            reduce_copy(p, h, t).wait_send()
            gather_copy(p, h, t).wait_send()
        save_sum(p).wait()
    save_p3.wait()
    save_q1.wait()
    sent(*halo_p1)
    sent(*halo_q3)
    sent(*halo_p2)
    sent(*halo_q2)


def store_kernel(a, b, c, out_a, out_b, out_c, sem):
    copies = [
        pltpu.make_async_copy(src, dst, sem.at[i])
        for i, (src, dst) in enumerate(((a, out_a), (b, out_b), (c, out_c)))
    ]
    for copy in copies:
        copy.start()
    for copy in copies:
        copy.wait()


def shards(
    coefficient,
    fwd_older,
    fwd_recent,
    adj_later,
    adj_recent,
    source_xcell,
    source_ycell,
    source_zcell,
    amplitude,
    receiver_xcell,
    receiver_ycell,
    receiver_zcell,
    observed,
):
    ndom, nshot = lax.axis_size("dom"), lax.axis_size("shot")
    nx, ny, nz = coefficient.shape
    cells = nx * ny
    bits = nshot.bit_length() - 1
    rows = CH * ny
    field = jax.ShapeDtypeStruct((nx, ny, nz), jnp.float32)
    plane_out = jax.ShapeDtypeStruct((cells, nz), jnp.float32)
    parts = 2 * (nx // CH)
    while parts > 1 and (cells // parts) // nshot < 8:
        parts //= 2
    hbm = pl.BlockSpec(memory_space=pltpu.HBM)
    vmem = pl.BlockSpec(memory_space=pltpu.VMEM)
    smem = pl.BlockSpec(memory_space=pltpu.SMEM)
    block = pltpu.VMEM((nx, ny, nz), jnp.float32)
    wide = pltpu.VMEM((nx + 2 * R, ny, nz), jnp.float32)
    plane = pltpu.VMEM((cells, nz), jnp.float32)
    p3, q1, grad = pl.pallas_call(
        functools.partial(kernel, (ndom, nshot)),
        out_shape=(field, field, plane_out),
        in_specs=[hbm] * 5 + [smem] * 4 + [vmem] * 4,
        out_specs=(hbm,) * 3,
        scratch_shapes=[block] * 2
        + [plane]
        + [block] * 3
        + [wide] * 4
        + [pltpu.VMEM((2 * nz, nz), jnp.bfloat16), pltpu.VMEM((rows, 2 * rows), jnp.bfloat16)]
        + [plane] * 5
        + [
            pltpu.SemaphoreType.DMA((5,)),
            pltpu.SemaphoreType.DMA((2 + parts,)),
            pltpu.SemaphoreType.DMA((4, 2)),
            pltpu.SemaphoreType.DMA((4, 2)),
            pltpu.SemaphoreType.DMA((parts, 2 * bits)),
            pltpu.SemaphoreType.DMA((parts, 2 * bits)),
        ],
        compiler_params=pltpu.CompilerParams(
            collective_id=0, has_side_effects=True, vmem_limit_bytes=60 * 1024 * 1024
        ),
        cost_estimate=pl.CostEstimate(flops=4 * 10**9, bytes_accessed=8 * 4 * cells * nz, transcendentals=0),
        name="wave_steps",
    )(
        coefficient,
        fwd_older[0],
        fwd_recent[0],
        adj_later[0],
        adj_recent[0],
        source_xcell,
        source_ycell,
        source_zcell,
        amplitude,
        receiver_xcell,
        receiver_ycell,
        receiver_zcell,
        observed[0],
    )
    p3, q1, grad = pl.pallas_call(
        store_kernel,
        out_shape=(field, field, plane_out),
        in_specs=[hbm] * 3,
        out_specs=(hbm,) * 3,
        scratch_shapes=[pltpu.SemaphoreType.DMA((3,))],
        compiler_params=pltpu.CompilerParams(vmem_limit_bytes=60 * 1024 * 1024),
        cost_estimate=pl.CostEstimate(flops=0, bytes_accessed=6 * 4 * cells * nz, transcendentals=0),
        name="store_results",
    )(p3, q1, grad)
    return p3[None], q1[None], grad.reshape(nx, ny, nz)


def solution(mesh):
    return jax.shard_map(
        shards,
        mesh=mesh,
        in_specs=(
            P("dom", None, None),
            P("shot", "dom", None, None),
            P("shot", "dom", None, None),
            P("shot", "dom", None, None),
            P("shot", "dom", None, None),
            P("shot"),
            P("shot"),
            P("shot"),
            P("shot", None),
            P("shot", None),
            P("shot", None),
            P("shot", None),
            P("shot", None, None),
        ),
        out_specs=(
            P("shot", "dom", None, None),
            P("shot", "dom", None, None),
            P("dom", None, None),
        ),
        check_vma=False,
    )
```

time: 199 us -> 121 us (0.61)
  Pallas kernels: 0 us -> 118 us
  waiting for transfers between devices: 79.8 us -> 0 us
  other arithmetic: 35.3 us -> 0 us
  local copies, waits for them, and re-layouts: 34.5 us -> 0 us
  starting transfers between devices: 20.6 us -> 0 us
  between operations: 20.4 us -> 2.58 us
  blocking collectives: 7.5 us -> 0 us
    pallas_call x0 -> x2, Pallas kernels: none -> 118 us  [the longest x1 72.6 us: shards(): pl.pallas_call(store_kernel, out_shape=(field, field, plane_out), in_spec...]
    psum x1 -> x0, waiting for transfers between devices: 78.9 us -> none  [shards(): gradient = lax.psum(early_term + late_term, 'shot')]
    gather x2 -> x0, local copies, waits for them, and re-layouts: 21.1 us -> none  [sample(): picked = field[local, ycells, zcells]]
    add x8 -> x0, other arithmetic: 21 us -> none  [the longest x4 12.4 us: laplace_core(): total + weight * (padded[:, R:R + width_y, R + offset:R + offset + width_...]
    ppermute x8 -> x0, starting transfers between devices: 20.6 us -> none  [the longest x4 15.4 us: with_halo(): lax.ppermute(lax.slice_in_dim(block, block.shape[dim] - width, None, axis...]
    unnamed x5 -> x0, other arithmetic: 12.9 us -> none
    psum x1 -> x0, blocking collectives: 7.5 us -> none  [shards(): traces = lax.psum(samples, 'dom')]
    slice x7 -> x0, local copies, waits for them, and re-layouts: 4.52 us -> none  [the longest x4 3.33 us: with_halo(): lax.slice_in_dim(block, 0, width, axis=dim)]
  transfers between devices with their start and end apart: 9 -> 0, of which waited for: 2 -> 0; matrix products, arithmetic and copies ran while one was open for 11% -> 0% of each run, Pallas kernels for 0% -> 0%
where the time goes in v2:
time: 121 us
  Pallas kernels  118 us (98%)
  between operations  2.58 us (2%)
    pallas_call x1, Pallas kernels, shards(): pl.pallas_call(store_kernel, out_shape=(field, field, plane_out), in_spec...  72.6 us
    pallas_call x1, Pallas kernels, shards(): pl.pallas_call(functools.partial(kernel, (ndom, nshot)), out_shape=(field...  45.3 us

profile of v2, /device:TPU:0, one launch (start us, length us, event | category | flops | bytes accessed | tf_op | source)
XLA Modules:
  0.0 120.5 jit_solution(11949607813283818183)
XLA Ops:
  2.6 45.3 %wave_steps.1 = (f32[32,16,384]{2,1,0:T(8,128)}, f32[32,16,384]{2,1,0:T(8,128)}, f32[512,384]{1,0:T(8,128)}) custom-call(f32[32,16,384]{2,1,0:T(8,128)} %coef_in.1, f32[32,16,384]{2,1,0:T(8,128)} %bitcast.8, f32[32,16,384]{2,1,0:T(8,128)} %bitcast.9, f32[32,16,384]{2,1,0:T(8,128)} %bitcast.10, f32[32,16,384]{2,1,0:T(8,128)} %bitcast.11, s32[1]{0:T(128)S(6)} %copy.16.sx, ...), custom_call_target="tpu_custom_call" | custom-call | flops 4000000000 | bytes 6291456 | tf_op jit(solution)/shard_map/wave_steps/pallas_call | solution.py:428
  47.9 72.6 %store_results.1 = (f32[32,16,384]{2,1,0:T(8,128)}, f32[32,16,384]{2,1,0:T(8,128)}, f32[512,384]{1,0:T(8,128)}) custom-call(f32[32,16,384]{2,1,0:T(8,128)} %get-tuple-element.9.a, f32[32,16,384]{2,1,0:T(8,128)} %get-tuple-element.10.b, f32[512,384]{1,0:T(8,128)} %get-tuple-element.11.c), custom_call_target="tpu_custom_call" | custom-call | bytes 4718592 | tf_op jit(solution)/shard_map/store_results/pallas_call | solution.py:467

commit v3 on v2

--- a/solution.py
+++ b/solution.py
@@ -73,7 +73,8 @@
     ndom, nshot = dims
     nx, ny, nz = coef.shape
     rows = CH * ny
-    nch = nx // CH
+    npair = nx // CH
+    slab = R * ny
     bits = nshot.bit_length() - 1
     parts = gsend.shape[0]
     prow = nx * ny // parts
@@ -195,12 +196,19 @@
         high = value.astype(jnp.bfloat16).astype(jnp.float32)
         return spread(high) + spread(value - high)
 
+    def slabs(c):
+        return c * R, nx - R - c * R
+
     def laplace(ref, c):
-        ext = ref[pl.ds(c * CH, CH + 2 * R)]
-        center = ext[R : R + CH]
+        sides = [ref[pl.ds(first, 3 * R)] for first in slabs(c)]
+
+        def shifted(k):
+            return jnp.concatenate([side[R + k : 2 * R + k] for side in sides], axis=0)
+
+        center = shifted(0)
         total = W0 * center
         for k, weight in enumerate(WK, 1):
-            total = total + weight * (ext[R + k : R + k + CH] + ext[R - k : R - k + CH])
+            total = total + weight * (shifted(k) + shifted(-k))
         flat = center.reshape(rows, nz)
         high = flat.astype(jnp.bfloat16)
         low = (flat - high.astype(jnp.float32)).astype(jnp.bfloat16)
@@ -208,20 +216,26 @@
         along_y = jnp.dot(yy[...], jnp.concatenate([high, low], axis=0), preferred_element_type=jnp.float32)
         return (total.reshape(rows, nz) + (along_z + along_y)) * (1.0 / SCALE)
 
-    def flat(ref, c, first=0):
-        return ref[pl.ds(first + c * CH, CH)].reshape(rows, nz)
-
-    def put(ref, c, value, first=0):
-        ref[pl.ds(first + c * CH, CH)] = value.reshape(CH, ny, nz)
-
-    def at(c):
-        return pl.ds(pl.multiple_of(c * rows, rows), rows)
+    def flat(ref, c, skip=0):
+        return jnp.concatenate([ref[pl.ds(skip + first, R)] for first in slabs(c)], axis=0).reshape(rows, nz)
+
+    def put(ref, c, value, skip=0):
+        value = value.reshape(CH, ny, nz)
+        for i, first in enumerate(slabs(c)):
+            ref[pl.ds(skip + first, R)] = value[i * R : (i + 1) * R]
+
+    def slab_rows(first):
+        return pl.ds(pl.multiple_of(first * ny, slab), slab)
+
+    def take(ref, c):
+        return jnp.concatenate([ref[slab_rows(first), :] for first in slabs(c)], axis=0)
 
     srow = (sx[0] - base) * ny + sy[0]
     szed = sz[0]
 
     def source(c, t):
-        row = lax.broadcasted_iota(jnp.int32, (rows, 1), 0) + c * rows
+        row = lax.broadcasted_iota(jnp.int32, (rows, 1), 0)
+        row = row + jnp.where(row < slab, c * slab, (nx - CH - c * R) * ny)
         lane = lax.broadcasted_iota(jnp.int32, (1, nz), 1)
         return jnp.where(row == srow, amp[0, t], 0.0) * jnp.where(lane == szed, 1.0, 0.0)
 
@@ -234,31 +248,22 @@
         put(p3, c, value)
 
     def step_q2(c):
-        points = cnt[at(c), :] * flat(p3, c) - o3[at(c), :]
+        points = take(cnt, c) * flat(p3, c) - take(o3, c)
         value = 2.0 * flat(q3, c, R) - flat(later, c) + flat(coef, c) * (laplace(q3, c) + points)
         put(q2, c, value, R)
 
     def step_q1(c):
         two = flat(p2, c, R)
-        points = cnt[at(c), :] * two - o2[at(c), :]
+        points = take(cnt, c) * two - take(o2, c)
         now = flat(q2, c, R)
         value = 2.0 * now - flat(q3, c, R) + flat(coef, c) * (laplace(q2, c) + points)
         put(q1, c, value)
         one = flat(p1, c, R)
         early = two - 2.0 * one + flat(older, c)
         late = flat(p3, c) - 2.0 * two + one
-        grad[at(c), :] = value * early + now * late
-
-    def sweep(before_edges, body):
-        def turn(i, carry):
-            @pl.when(i == nch - 2)
-            def _():
-                before_edges()
-
-            body(lax.rem(i + 1, nch))
-            return carry
-
-        lax.fori_loop(0, nch, turn, 0)
+        term = value * early + now * late
+        for i, first in enumerate(slabs(c)):
+            grad[slab_rows(first), :] = term[i * slab : (i + 1) * slab]
 
     def order_of(h):
         order = list(range(bits))
@@ -324,57 +329,95 @@
             else:
                 save_sum(p).start()
 
+    early_start = parts == 2 * npair
+
+    def group(c):
+        return ((c, 0), (parts - 1 - c, c % 2)) if early_start else ((c, c % 2),)
+
     cnt[...] = spread(1.0)
     o3[...] = observe(1)
     for copy in loads[:3]:
         copy.wait()
-    sweep(lambda: receive(*halo_p1), step_p2)
+
+    def first_turn(i, carry):
+        @pl.when(i == npair - 1)
+        def _():
+            receive(*halo_p1)
+
+        step_p2(npair - 1 - i)
+        return carry
+
+    lax.fori_loop(0, npair, first_turn, 0)
     send(*halo_p2)
     o2[...] = observe(0)
     for copy in loads[3:]:
         copy.wait()
 
-    def middle(c):
-        step_p3(c)
-        step_q2(c)
-
-    def arrive():
-        receive(*halo_q3)
-        receive(*halo_p2)
-
-    sweep(arrive, middle)
-    send(*halo_q2)
     save_p3 = pltpu.make_async_copy(p3, out_p3, save.at[0])
     save_q1 = pltpu.make_async_copy(q1, out_q1, save.at[1])
-    save_p3.start()
-    per = max(parts // nch, 1)
-
-    def last(c):
-        step_q1(c)
-        if parts >= nch:
-            for h in range(per):
-                reduce_copy(c * per + h, h % 2, 0).start()
-
-    sweep(lambda: receive(*halo_q2), last)
+
+    def turn(i, carry):
+        @pl.when(i == npair - 1)
+        def _():
+            receive(*halo_q3)
+            receive(*halo_p2)
+
+        @pl.when(i < npair)
+        def _():
+            step_p3(npair - 1 - i)
+            step_q2(npair - 1 - i)
+
+        @pl.when(i == npair - 1)
+        def _():
+            send(*halo_q2)
+            save_p3.start()
+
+        @pl.when(i == npair)
+        def _():
+            receive(*halo_q2)
+
+        @pl.when(i > 0)
+        def _():
+            step_q1(npair - i)
+
+        if early_start:
+            for c in range(npair):
+
+                @pl.when(i == npair - c)
+                def _():
+                    for p, h in group(c):
+                        reduce_copy(p, h, 0).start()
+
+                for n in range(c):
+
+                    @pl.when(i == npair - c + 1 + n)
+                    def _():
+                        for p, h in group(c):
+                            advance(p, h, n)
+
+        return carry
+
+    lax.fori_loop(0, npair + 1, turn, 0)
     save_q1.start()
-    if parts < nch:
-        for p in range(parts):
-            reduce_copy(p, p % 2, 0).start()
-    groups = [[(((c + 1) % nch) * per + h, h % 2) for h in range(per)] for c in range(nch)]
-    if parts < nch:
-        groups = [[(p, p % 2)] for p in range(parts)]
     steps = 2 * bits
-    for turn in range(steps + len(groups) - 1):
-        for g, group in enumerate(groups):
-            if 0 <= turn - g < steps:
-                for p, h in group:
-                    advance(p, h, turn - g)
-    for p in range(parts):
-        h = (p % per) % 2 if parts >= nch else p % 2
-        for t in range(bits):
-            reduce_copy(p, h, t).wait_send()
-            gather_copy(p, h, t).wait_send()
-        save_sum(p).wait()
+    if early_start:
+        left = [(c, c) for c in reversed(range(npair))]
+    else:
+        left = [(p, 0) for p in range(parts)]
+        for p, _ in left:
+            for portion in group(p):
+                reduce_copy(*portion, 0).start()
+    while left:
+        for c, n in left:
+            for p, h in group(c):
+                advance(p, h, n)
+        left = [(c, n + 1) for c, n in left if n + 1 < steps]
+    for c in range(npair if early_start else parts):
+        for p, h in group(c):
+            for t in range(bits):
+                reduce_copy(p, h, t).wait_send()
+                gather_copy(p, h, t).wait_send()
+            save_sum(p).wait()
     save_p3.wait()
     save_q1.wait()
     sent(*halo_p1)
@@ -383,15 +426,22 @@
     sent(*halo_q2)
 
 
-def store_kernel(a, b, c, out_a, out_b, out_c, sem):
-    copies = [
-        pltpu.make_async_copy(src, dst, sem.at[i])
-        for i, (src, dst) in enumerate(((a, out_a), (b, out_b), (c, out_c)))
-    ]
-    for copy in copies:
-        copy.start()
-    for copy in copies:
-        copy.wait()
+def store_kernel(a, b, c, out_a, out_b, out_c, va, vb, vc, sem):
+    pieces = 2
+    moves = []
+    for i in range(pieces):
+        for k, (src, mid, dst) in enumerate(((a, va, out_a), (b, vb, out_b), (c, vc, out_c))):
+            size = src.shape[0] // pieces
+            part = pl.ds(i * size, size)
+            come = pltpu.make_async_copy(src.at[part], mid.at[part], sem.at[0, i, k])
+            go = pltpu.make_async_copy(mid.at[part], dst.at[part], sem.at[1, i, k])
+            come.start()
+            moves.append((come, go))
+    for come, go in moves:
+        come.wait()
+        go.start()
+    for come, go in moves:
+        go.wait()
 
 
 def shards(
@@ -469,7 +519,7 @@
         out_shape=(field, field, plane_out),
         in_specs=[hbm] * 3,
         out_specs=(hbm,) * 3,
-        scratch_shapes=[pltpu.SemaphoreType.DMA((3,))],
+        scratch_shapes=[block, block, plane, pltpu.SemaphoreType.DMA((2, 2, 3))],
         compiler_params=pltpu.CompilerParams(vmem_limit_bytes=60 * 1024 * 1024),
         cost_estimate=pl.CostEstimate(flops=0, bytes_accessed=6 * 4 * cells * nz, transcendentals=0),
         name="store_results",

time: 121 us -> 50.3 us (0.42)
  Pallas kernels: 118 us -> 47.5 us
    pallas_call x1, Pallas kernels: 72.6 us -> 2.49 us  [shards(): pl.pallas_call(store_kernel, out_shape=(field, field, plane_out), in_spec...]
where the time goes in v3:
time: 50.3 us; the launch traced here: 50.1 us
  Pallas kernels  47.5 us (94%)
  between operations  2.58 us (5%)
    pallas_call x1, Pallas kernels, shards(): pl.pallas_call(functools.partial(kernel, (ndom, nshot)), out_shape=(field...  45 us
    pallas_call x1, Pallas kernels, shards(): pl.pallas_call(store_kernel, out_shape=(field, field, plane_out), in_spec...  2.49 us

profile of v3, /device:TPU:0, one launch (start us, length us, event | category | flops | bytes accessed | tf_op | source)
XLA Modules:
  0.0 50.1 jit_solution(13136220494490532999)
XLA Ops:
  2.6 45.0 %wave_steps.1 = (f32[32,16,384]{2,1,0:T(8,128)}, f32[32,16,384]{2,1,0:T(8,128)}, f32[512,384]{1,0:T(8,128)}) custom-call(f32[32,16,384]{2,1,0:T(8,128)} %coef_in.1, f32[32,16,384]{2,1,0:T(8,128)} %bitcast.8, f32[32,16,384]{2,1,0:T(8,128)} %bitcast.9, f32[32,16,384]{2,1,0:T(8,128)} %bitcast.10, f32[32,16,384]{2,1,0:T(8,128)} %bitcast.11, s32[1]{0:T(128)S(6)} %copy.16.sx, ...), custom_call_target="tpu_custom_call" | custom-call | flops 4000000000 | bytes 6291456 | tf_op jit(solution)/shard_map/wave_steps/pallas_call | solution.py:478
  47.6 2.5 %store_results.1 = (f32[32,16,384]{2,1,0:T(8,128)}, f32[32,16,384]{2,1,0:T(8,128)}, f32[512,384]{1,0:T(8,128)}) custom-call(f32[32,16,384]{2,1,0:T(8,128)} %get-tuple-element.9.a, f32[32,16,384]{2,1,0:T(8,128)} %get-tuple-element.10.b, f32[512,384]{1,0:T(8,128)} %get-tuple-element.11.c), custom_call_target="tpu_custom_call" | custom-call | bytes 4718592 | tf_op jit(solution)/shard_map/store_results/pallas_call | solution.py:517

commit v4 on v3

--- a/solution.py
+++ b/solution.py
@@ -114,8 +114,6 @@
     def _():
         pl.semaphore_signal(barrier, inc=1, device_id={"dom": dom + 1}, device_id_type=MESH)
 
-    pl.semaphore_wait(barrier, bits + has_lo.astype(jnp.int32) + has_hi.astype(jnp.int32))
-
     def down(f, src, first, ref):
         return pltpu.make_async_remote_copy(
             src_ref=src.at[pl.ds(first, R)],
@@ -158,9 +156,6 @@
     halo_q3 = (Q3, adj_in, 0, q3)
     halo_p2 = (P2, p2, R, p2)
     halo_q2 = (Q2, q2, R, q2)
-    send(*halo_p1)
-    send(*halo_q3)
-
     zmat = band(nz, nz)
     zz[0:nz, :] = zmat
     zz[nz : 2 * nz, :] = zmat
@@ -187,34 +182,46 @@
     onz = lax.broadcasted_iota(jnp.int32, (nz, nrecv), 0) == rz[...]
     nt = (((1,), (1,)), ((), ()))
 
-    def spread(values):
-        side = jnp.where(onz, values, 0.0).astype(jnp.bfloat16)
-        return lax.dot_general(pick, side, nt, preferred_element_type=jnp.float32)
-
-    def observe(t):
+    def side(values):
+        return jnp.where(onz, values, 0.0).astype(jnp.bfloat16)
+
+    sides = [side(1.0)]
+    for t in (1, 0):
         value = obs[t : t + 1, :]
         high = value.astype(jnp.bfloat16).astype(jnp.float32)
-        return spread(high) + spread(value - high)
+        sides += [side(high), side(value - high)]
+    maps = lax.dot_general(pick, jnp.concatenate(sides, axis=0), nt, preferred_element_type=jnp.float32)
+    cnt[...] = maps[:, 0:nz]
+    o3[...] = maps[:, nz : 2 * nz] + maps[:, 2 * nz : 3 * nz]
+    o2[...] = maps[:, 3 * nz : 4 * nz] + maps[:, 4 * nz : 5 * nz]
 
     def slabs(c):
         return c * R, nx - R - c * R
 
-    def laplace(ref, c):
-        sides = [ref[pl.ds(first, 3 * R)] for first in slabs(c)]
-
-        def shifted(k):
-            return jnp.concatenate([side[R + k : 2 * R + k] for side in sides], axis=0)
-
-        center = shifted(0)
-        total = W0 * center
-        for k, weight in enumerate(WK, 1):
-            total = total + weight * (shifted(k) + shifted(-k))
-        flat = center.reshape(rows, nz)
-        high = flat.astype(jnp.bfloat16)
-        low = (flat - high.astype(jnp.float32)).astype(jnp.bfloat16)
+    def laplace(refs, c):
+        totals, highs, lows = [], [], []
+        for ref in refs:
+            sides = [ref[pl.ds(first, 3 * R)] for first in slabs(c)]
+
+            def shifted(k):
+                return jnp.concatenate([side[R + k : 2 * R + k] for side in sides], axis=0)
+
+            center = shifted(0)
+            total = W0 * center
+            for k, weight in enumerate(WK, 1):
+                total = total + weight * (shifted(k) + shifted(-k))
+            totals.append(total.reshape(rows, nz))
+            center = center.reshape(rows, nz)
+            highs.append(center.astype(jnp.bfloat16))
+            lows.append((center - highs[-1].astype(jnp.float32)).astype(jnp.bfloat16))
+        high, low = jnp.concatenate(highs, axis=0), jnp.concatenate(lows, axis=0)
         along_z = jnp.dot(jnp.concatenate([high, low], axis=1), zz[...], preferred_element_type=jnp.float32)
+        high, low = jnp.concatenate(highs, axis=1), jnp.concatenate(lows, axis=1)
         along_y = jnp.dot(yy[...], jnp.concatenate([high, low], axis=0), preferred_element_type=jnp.float32)
-        return (total.reshape(rows, nz) + (along_z + along_y)) * (1.0 / SCALE)
+        return [
+            (total + (along_z[i * rows : (i + 1) * rows] + along_y[:, i * nz : (i + 1) * nz])) * (1.0 / SCALE)
+            for i, total in enumerate(totals)
+        ]
 
     def flat(ref, c, skip=0):
         return jnp.concatenate([ref[pl.ds(skip + first, R)] for first in slabs(c)], axis=0).reshape(rows, nz)
@@ -240,23 +247,24 @@
         return jnp.where(row == srow, amp[0, t], 0.0) * jnp.where(lane == szed, 1.0, 0.0)
 
     def step_p2(c):
-        value = 2.0 * flat(p1, c, R) - flat(older, c) + flat(coef, c) * (laplace(p1, c) + source(c, 0))
+        (change,) = laplace([p1], c)
+        value = 2.0 * flat(p1, c, R) - flat(older, c) + flat(coef, c) * (change + source(c, 0))
         put(p2, c, value, R)
 
-    def step_p3(c):
-        value = 2.0 * flat(p2, c, R) - flat(p1, c, R) + flat(coef, c) * (laplace(p2, c) + source(c, 1))
+    def step_p3_q2(c):
+        change_p, change_q = laplace([p2, q3], c)
+        scale = flat(coef, c)
+        value = 2.0 * flat(p2, c, R) - flat(p1, c, R) + scale * (change_p + source(c, 1))
         put(p3, c, value)
-
-    def step_q2(c):
-        points = take(cnt, c) * flat(p3, c) - take(o3, c)
-        value = 2.0 * flat(q3, c, R) - flat(later, c) + flat(coef, c) * (laplace(q3, c) + points)
+        points = take(cnt, c) * value - take(o3, c)
+        value = 2.0 * flat(q3, c, R) - flat(later, c) + scale * (change_q + points)
         put(q2, c, value, R)
 
     def step_q1(c):
         two = flat(p2, c, R)
         points = take(cnt, c) * two - take(o2, c)
         now = flat(q2, c, R)
-        value = 2.0 * now - flat(q3, c, R) + flat(coef, c) * (laplace(q2, c) + points)
+        value = 2.0 * now - flat(q3, c, R) + flat(coef, c) * (laplace([q2], c)[0] + points)
         put(q1, c, value)
         one = flat(p1, c, R)
         early = two - 2.0 * one + flat(older, c)
@@ -332,24 +340,19 @@
     early_start = parts == 2 * npair
 
     def group(c):
-        return ((c, 0), (parts - 1 - c, c % 2)) if early_start else ((c, c % 2),)
-
-    cnt[...] = spread(1.0)
-    o3[...] = observe(1)
+        return ((c, 0), (parts - 1 - c, (c + 1) % 2)) if early_start else ((c, c % 2),)
+
+    pl.semaphore_wait(barrier, bits + has_lo.astype(jnp.int32) + has_hi.astype(jnp.int32))
+    send(*halo_p1)
+    send(*halo_q3)
     for copy in loads[:3]:
         copy.wait()
 
     def first_turn(i, carry):
-        @pl.when(i == npair - 1)
-        def _():
-            receive(*halo_p1)
-
         step_p2(npair - 1 - i)
         return carry
 
-    lax.fori_loop(0, npair, first_turn, 0)
-    send(*halo_p2)
-    o2[...] = observe(0)
+    lax.fori_loop(0, npair - 1, first_turn, 0)
     for copy in loads[3:]:
         copy.wait()
 
@@ -359,13 +362,18 @@
     def turn(i, carry):
         @pl.when(i == npair - 1)
         def _():
+            receive(*halo_p2)
+
+        @pl.when(i < npair)
+        def _():
+            step_p3_q2(npair - 1 - i)
+
+        @pl.when(i == max(npair - 3, 0))
+        def _():
+            receive(*halo_p1)
             receive(*halo_q3)
-            receive(*halo_p2)
-
-        @pl.when(i < npair)
-        def _():
-            step_p3(npair - 1 - i)
-            step_q2(npair - 1 - i)
+            step_p2(0)
+            send(*halo_p2)
 
         @pl.when(i == npair - 1)
         def _():

time: 50.3 us -> 48.7 us (0.968)
  Pallas kernels: 47.5 us -> 45.9 us
    pallas_call x1, Pallas kernels: 45 us -> 43.4 us  [shards(): pl.pallas_call(functools.partial(kernel, (ndom, nshot)), out_shape=(field...]
where the time goes in v4:
time: 48.7 us; the launch traced here: 48.4 us
  Pallas kernels  45.9 us (94%)
  between operations  2.58 us (5%)
    pallas_call x1, Pallas kernels, shards(): pl.pallas_call(functools.partial(kernel, (ndom, nshot)), out_shape=(field...  43.4 us
    pallas_call x1, Pallas kernels, shards(): pl.pallas_call(store_kernel, out_shape=(field, field, plane_out), in_spec...  2.49 us

profile of v4, /device:TPU:0, one launch (start us, length us, event | category | flops | bytes accessed | tf_op | source)
XLA Modules:
  0.0 48.4 jit_solution(7453253801421736236)
XLA Ops:
  2.6 43.4 %wave_steps.1 = (f32[32,16,384]{2,1,0:T(8,128)}, f32[32,16,384]{2,1,0:T(8,128)}, f32[512,384]{1,0:T(8,128)}) custom-call(f32[32,16,384]{2,1,0:T(8,128)} %coef_in.1, f32[32,16,384]{2,1,0:T(8,128)} %bitcast.8, f32[32,16,384]{2,1,0:T(8,128)} %bitcast.9, f32[32,16,384]{2,1,0:T(8,128)} %bitcast.10, f32[32,16,384]{2,1,0:T(8,128)} %bitcast.11, s32[1]{0:T(128)S(6)} %copy.16.sx, ...), custom_call_target="tpu_custom_call" | custom-call | flops 4000000000 | bytes 6291456 | tf_op jit(solution)/shard_map/wave_steps/pallas_call | solution.py:486
  46.0 2.5 %store_results.1 = (f32[32,16,384]{2,1,0:T(8,128)}, f32[32,16,384]{2,1,0:T(8,128)}, f32[512,384]{1,0:T(8,128)}) custom-call(f32[32,16,384]{2,1,0:T(8,128)} %get-tuple-element.9.a, f32[32,16,384]{2,1,0:T(8,128)} %get-tuple-element.10.b, f32[512,384]{1,0:T(8,128)} %get-tuple-element.11.c), custom_call_target="tpu_custom_call" | custom-call | bytes 4718592 | tf_op jit(solution)/shard_map/store_results/pallas_call | solution.py:525

commit v5 on v4

--- a/solution.py
+++ b/solution.py
@@ -43,9 +43,6 @@
     ry,
     rz,
     obs,
-    out_p3,
-    out_q1,
-    out_g,
     p3,
     q1,
     gsum,
@@ -64,7 +61,6 @@
     grad,
     land,
     load,
-    save,
     hsend,
     hrecv,
     gsend,
@@ -270,8 +266,7 @@
         early = two - 2.0 * one + flat(older, c)
         late = flat(p3, c) - 2.0 * two + one
         term = value * early + now * late
-        for i, first in enumerate(slabs(c)):
-            grad[slab_rows(first), :] = term[i * slab : (i + 1) * slab]
+        grad[pl.ds(pl.multiple_of(c * rows, rows), rows), :] = term
 
     def order_of(h):
         order = list(range(bits))
@@ -314,9 +309,6 @@
             device_id={"shot": partner[order_of(h)[t]]},
             device_id_type=MESH,
         )
-
-    def save_sum(p):
-        return pltpu.make_async_copy(gsum.at[rows_at(p * prow, prow)], out_g.at[rows_at(p * prow, prow)], save.at[2 + p])
 
     def advance(p, h, n):
         if n < bits:
@@ -334,13 +326,11 @@
             gather_copy(p, h, t).wait_recv()
             if t:
                 gather_copy(p, h, t - 1).start()
-            else:
-                save_sum(p).start()
-
-    early_start = parts == 2 * npair
+
+    early_start = parts == npair
 
     def group(c):
-        return ((c, 0), (parts - 1 - c, (c + 1) % 2)) if early_start else ((c, c % 2),)
+        return ((c, (c + 1) % 2),)
 
     pl.semaphore_wait(barrier, bits + has_lo.astype(jnp.int32) + has_hi.astype(jnp.int32))
     send(*halo_p1)
@@ -356,9 +346,6 @@
     for copy in loads[3:]:
         copy.wait()
 
-    save_p3 = pltpu.make_async_copy(p3, out_p3, save.at[0])
-    save_q1 = pltpu.make_async_copy(q1, out_q1, save.at[1])
-
     def turn(i, carry):
         @pl.when(i == npair - 1)
         def _():
@@ -378,7 +365,6 @@
         @pl.when(i == npair - 1)
         def _():
             send(*halo_q2)
-            save_p3.start()
 
         @pl.when(i == npair)
         def _():
@@ -406,7 +392,6 @@
         return carry
 
     lax.fori_loop(0, npair + 1, turn, 0)
-    save_q1.start()
     steps = 2 * bits
     if early_start:
         left = [(c, c) for c in reversed(range(npair))]
@@ -425,31 +410,24 @@
             for t in range(bits):
                 reduce_copy(p, h, t).wait_send()
                 gather_copy(p, h, t).wait_send()
-            save_sum(p).wait()
-    save_p3.wait()
-    save_q1.wait()
     sent(*halo_p1)
     sent(*halo_q3)
     sent(*halo_p2)
     sent(*halo_q2)
 
 
-def store_kernel(a, b, c, out_a, out_b, out_c, va, vb, vc, sem):
-    pieces = 2
-    moves = []
-    for i in range(pieces):
-        for k, (src, mid, dst) in enumerate(((a, va, out_a), (b, vb, out_b), (c, vc, out_c))):
-            size = src.shape[0] // pieces
-            part = pl.ds(i * size, size)
-            come = pltpu.make_async_copy(src.at[part], mid.at[part], sem.at[0, i, k])
-            go = pltpu.make_async_copy(mid.at[part], dst.at[part], sem.at[1, i, k])
-            come.start()
-            moves.append((come, go))
-    for come, go in moves:
-        come.wait()
-        go.start()
-    for come, go in moves:
-        go.wait()
+def store_kernel(a, b, c, out_a, out_b, out_c, sem):
+    moves = [(a, out_a), (b, out_b)]
+    slab = R * out_a.shape[1]
+    count = c.shape[0] // slab
+    for i in range(count):
+        to = i // 2 if i % 2 == 0 else count - 1 - i // 2
+        moves.append((c.at[pl.ds(i * slab, slab)], out_c.at[pl.ds(to * slab, slab)]))
+    copies = [pltpu.make_async_copy(src, dst, sem.at[i]) for i, (src, dst) in enumerate(moves)]
+    for copy in copies:
+        copy.start()
+    for copy in copies:
+        copy.wait()
 
 
 def shards(
@@ -474,7 +452,7 @@
     rows = CH * ny
     field = jax.ShapeDtypeStruct((nx, ny, nz), jnp.float32)
     plane_out = jax.ShapeDtypeStruct((cells, nz), jnp.float32)
-    parts = 2 * (nx // CH)
+    parts = nx // CH
     while parts > 1 and (cells // parts) // nshot < 8:
         parts //= 2
     hbm = pl.BlockSpec(memory_space=pltpu.HBM)
@@ -487,23 +465,20 @@
         functools.partial(kernel, (ndom, nshot)),
         out_shape=(field, field, plane_out),
         in_specs=[hbm] * 5 + [smem] * 4 + [vmem] * 4,
-        out_specs=(hbm,) * 3,
-        scratch_shapes=[block] * 2
-        + [plane]
-        + [block] * 3
+        out_specs=(vmem,) * 3,
+        scratch_shapes=[block] * 3
         + [wide] * 4
         + [pltpu.VMEM((2 * nz, nz), jnp.bfloat16), pltpu.VMEM((rows, 2 * rows), jnp.bfloat16)]
         + [plane] * 5
         + [
             pltpu.SemaphoreType.DMA((5,)),
-            pltpu.SemaphoreType.DMA((2 + parts,)),
             pltpu.SemaphoreType.DMA((4, 2)),
             pltpu.SemaphoreType.DMA((4, 2)),
             pltpu.SemaphoreType.DMA((parts, 2 * bits)),
             pltpu.SemaphoreType.DMA((parts, 2 * bits)),
         ],
         compiler_params=pltpu.CompilerParams(
-            collective_id=0, has_side_effects=True, vmem_limit_bytes=60 * 1024 * 1024
+            collective_id=0, has_side_effects=True, vmem_limit_bytes=51 * 1024 * 1024
         ),
         cost_estimate=pl.CostEstimate(flops=4 * 10**9, bytes_accessed=8 * 4 * cells * nz, transcendentals=0),
         name="wave_steps",
@@ -525,10 +500,10 @@
     p3, q1, grad = pl.pallas_call(
         store_kernel,
         out_shape=(field, field, plane_out),
-        in_specs=[hbm] * 3,
+        in_specs=[vmem] * 3,
         out_specs=(hbm,) * 3,
-        scratch_shapes=[block, block, plane, pltpu.SemaphoreType.DMA((2, 2, 3))],
-        compiler_params=pltpu.CompilerParams(vmem_limit_bytes=60 * 1024 * 1024),
+        scratch_shapes=[pltpu.SemaphoreType.DMA((2 + nx // R,))],
+        compiler_params=pltpu.CompilerParams(vmem_limit_bytes=16 * 1024 * 1024),
         cost_estimate=pl.CostEstimate(flops=0, bytes_accessed=6 * 4 * cells * nz, transcendentals=0),
         name="store_results",
     )(p3, q1, grad)

time: 48.7 us -> 53.6 us (1.10)
  Pallas kernels: 45.9 us -> 48.7 us
  local copies, waits for them, and re-layouts: 0 us -> 2.04 us
    pallas_call x1, Pallas kernels: 43.4 us -> 47.2 us  [shards(): pl.pallas_call(functools.partial(kernel, (ndom, nshot)), out_shape=(field...]
    unnamed x0 -> x10, local copies, waits for them, and re-layouts: none -> 2.04 us
    pallas_call x1, Pallas kernels: 2.49 us -> 1.47 us  [shards(): pl.pallas_call(store_kernel, out_shape=(field, field, plane_out), in_spec...]
where the time goes in v5:
time: 53.6 us; the launch traced here: 53.3 us
  Pallas kernels  48.7 us (91%)
  between operations  2.63 us (5%)
  local copies, waits for them, and re-layouts  2.04 us (4%)
    pallas_call x1, Pallas kernels, shards(): pl.pallas_call(functools.partial(kernel, (ndom, nshot)), out_shape=(field...  47.2 us
    unnamed x10, local copies, waits for them, and re-layouts  2.04 us
    pallas_call x1, Pallas kernels, shards(): pl.pallas_call(store_kernel, out_shape=(field, field, plane_out), in_spec...  1.47 us

profile of v5, /device:TPU:0, one launch (start us, length us, event | category | flops | bytes accessed | tf_op | source)
XLA Modules:
  0.0 53.3 jit_solution(4382025979933791778)
XLA Ops:
  0.6 0.0 copy-start
  2.6 0.0 copy-start.1
  2.6 0.0 copy-start.4
  2.6 0.0 copy-done
  2.6 0.7 %copy-done.1 = s32[1,1024]{1,0:T(1,128)S(1)} copy-done((s32[1,1024]{1,0:T(1,128)S(1)}, s32[1,1024]{1,0:T(1,128)}, u32[]{:S(2)}) %copy-start.1) | copy-done | bytes 4120
  3.3 0.0 copy-done.4
  3.3 0.0 copy-start.2
  3.3 0.7 %copy-done.2 = s32[1,1024]{1,0:T(1,128)S(1)} copy-done((s32[1,1024]{1,0:T(1,128)S(1)}, s32[1,1024]{1,0:T(1,128)}, u32[]{:S(2)}) %copy-start.2) | copy-done | bytes 4120
  4.0 0.0 copy-start.3
  4.0 0.7 %copy-done.3 = s32[1,1024]{1,0:T(1,128)S(1)} copy-done((s32[1,1024]{1,0:T(1,128)S(1)}, s32[1,1024]{1,0:T(1,128)}, u32[]{:S(2)}) %copy-start.3) | copy-done | bytes 4120
  4.7 47.2 %wave_steps.1 = (f32[32,16,384]{2,1,0:T(8,128)S(1)}, f32[32,16,384]{2,1,0:T(8,128)S(1)}, f32[512,384]{1,0:T(8,128)S(1)}) custom-call(f32[32,16,384]{2,1,0:T(8,128)} %coef_in.1, f32[32,16,384]{2,1,0:T(8,128)} %bitcast.9, f32[32,16,384]{2,1,0:T(8,128)} %bitcast.10, f32[32,16,384]{2,1,0:T(8,128)} %bitcast.11, f32[32,16,384]{2,1,0:T(8,128)} %bitcast.12, ...), custom_call_target="tpu_custom_call" | custom-call | flops 4000000000 | bytes 6291456 | tf_op jit(solution)/shard_map/wave_steps/pallas_call | solution.py:464
  51.9 1.5 %store_results.1 = (f32[32,16,384]{2,1,0:T(8,128)}, f32[32,16,384]{2,1,0:T(8,128)}, f32[512,384]{1,0:T(8,128)}) custom-call(f32[32,16,384]{2,1,0:T(8,128)S(1)} %get-tuple-element.9.a, f32[32,16,384]{2,1,0:T(8,128)S(1)} %get-tuple-element.10.b, f32[512,384]{1,0:T(8,128)S(1)} %get-tuple-element.11.c), custom_call_target="tpu_custom_call" | custom-call | bytes 4718592 | tf_op jit(solution)/shard_map/store_results/pallas_call | solution.py:500
Async XLA Ops:
  0.6 2.0 %copy-start = (f32[1,2,1024]{2,1,0:T(2,128)S(1)}, f32[1,2,1024]{2,1,0:T(2,128)}, u32[]{:S(2)}) copy-start(f32[1,2,1024]{2,1,0:T(2,128)} %param.25) | copy-start | bytes 24580
  2.6 0.7 %copy-start.1 = (s32[1,1024]{1,0:T(1,128)S(1)}, s32[1,1024]{1,0:T(1,128)}, u32[]{:S(2)}) copy-start(s32[1,1024]{1,0:T(1,128)} %rx.1) | copy-start | bytes 12292
  2.6 0.7 %copy-start.4 = (f32[1,2]{1,0:T(1,128)S(1)}, f32[1,2]{1,0:T(1,128)}, u32[]{:S(2)}) copy-start(f32[1,2]{1,0:T(1,128)} %amp.1) | copy-start | bytes 28
  3.3 0.7 %copy-start.2 = (s32[1,1024]{1,0:T(1,128)S(1)}, s32[1,1024]{1,0:T(1,128)}, u32[]{:S(2)}) copy-start(s32[1,1024]{1,0:T(1,128)} %ry.1) | copy-start | bytes 12292
  4.0 0.7 %copy-start.3 = (s32[1,1024]{1,0:T(1,128)S(1)}, s32[1,1024]{1,0:T(1,128)}, u32[]{:S(2)}) copy-start(s32[1,1024]{1,0:T(1,128)} %rz.1) | copy-start | bytes 12292

commit v6 on v4

--- a/solution.py
+++ b/solution.py
@@ -396,9 +396,9 @@
                     for p, h in group(c):
                         reduce_copy(p, h, 0).start()
 
-                for n in range(c):
-
-                    @pl.when(i == npair - c + 1 + n)
+                for n in range(c - 1):
+
+                    @pl.when(i == npair - c + 2 + n)
                     def _():
                         for p, h in group(c):
                             advance(p, h, n)
@@ -409,7 +409,7 @@
     save_q1.start()
     steps = 2 * bits
     if early_start:
-        left = [(c, c) for c in reversed(range(npair))]
+        left = [(c, max(c - 1, 0)) for c in reversed(range(npair))]
     else:
         left = [(p, 0) for p in range(parts)]
         for p, _ in left:
@@ -435,7 +435,7 @@
 
 
 def store_kernel(a, b, c, out_a, out_b, out_c, va, vb, vc, sem):
-    pieces = 2
+    pieces = 4
     moves = []
     for i in range(pieces):
         for k, (src, mid, dst) in enumerate(((a, va, out_a), (b, vb, out_b), (c, vc, out_c))):
@@ -527,7 +527,7 @@
         out_shape=(field, field, plane_out),
         in_specs=[hbm] * 3,
         out_specs=(hbm,) * 3,
-        scratch_shapes=[block, block, plane, pltpu.SemaphoreType.DMA((2, 2, 3))],
+        scratch_shapes=[block, block, plane, pltpu.SemaphoreType.DMA((2, 4, 3))],
         compiler_params=pltpu.CompilerParams(vmem_limit_bytes=60 * 1024 * 1024),
         cost_estimate=pl.CostEstimate(flops=0, bytes_accessed=6 * 4 * cells * nz, transcendentals=0),
         name="store_results",

time: 48.7 us -> 47.1 us (0.967)
  Pallas kernels: 45.9 us -> 44.3 us
    pallas_call x1, Pallas kernels: 43.4 us -> 41.7 us  [shards(): pl.pallas_call(functools.partial(kernel, (ndom, nshot)), out_shape=(field...]
where the time goes in v6:
time: 47.1 us; the launch traced here: 46.9 us
  Pallas kernels  44.3 us (94%)
  between operations  2.58 us (5%)
    pallas_call x1, Pallas kernels, shards(): pl.pallas_call(functools.partial(kernel, (ndom, nshot)), out_shape=(field...  41.7 us
    pallas_call x1, Pallas kernels, shards(): pl.pallas_call(store_kernel, out_shape=(field, field, plane_out), in_spec...  2.62 us

profile of v6, /device:TPU:0, one launch (start us, length us, event | category | flops | bytes accessed | tf_op | source)
XLA Modules:
  0.0 46.9 jit_solution(15572042556515202998)
XLA Ops:
  2.6 41.7 %wave_steps.1 = (f32[32,16,384]{2,1,0:T(8,128)}, f32[32,16,384]{2,1,0:T(8,128)}, f32[512,384]{1,0:T(8,128)}) custom-call(f32[32,16,384]{2,1,0:T(8,128)} %coef_in.1, f32[32,16,384]{2,1,0:T(8,128)} %bitcast.8, f32[32,16,384]{2,1,0:T(8,128)} %bitcast.9, f32[32,16,384]{2,1,0:T(8,128)} %bitcast.10, f32[32,16,384]{2,1,0:T(8,128)} %bitcast.11, s32[1]{0:T(128)S(6)} %copy.16.sx, ...), custom_call_target="tpu_custom_call" | custom-call | flops 4000000000 | bytes 6291456 | tf_op jit(solution)/shard_map/wave_steps/pallas_call | solution.py:486
  44.2 2.6 %store_results.1 = (f32[32,16,384]{2,1,0:T(8,128)}, f32[32,16,384]{2,1,0:T(8,128)}, f32[512,384]{1,0:T(8,128)}) custom-call(f32[32,16,384]{2,1,0:T(8,128)} %get-tuple-element.9.a, f32[32,16,384]{2,1,0:T(8,128)} %get-tuple-element.10.b, f32[512,384]{1,0:T(8,128)} %get-tuple-element.11.c), custom_call_target="tpu_custom_call" | custom-call | bytes 4718592 | tf_op jit(solution)/shard_map/store_results/pallas_call | solution.py:525
